TPU v7x, 512 devices: a whole 4x4x16 slice. The times are simulated.
512 devices in a mesh: ctx: 64 (over x, z), dp: 8 (over y, core).
Axes of the slice: x: 4, y: 4, z: 16, core: 2. Of those that a mesh axis runs over, the one named last changes fastest.
Arguments:
- queries: bfloat16 [32768, 4096], P('ctx', 'dp'), may hold values from -6 to 6
- keys: bfloat16 [32768, 4096], P('ctx', 'dp'), may hold values from -0.5 to 0.5
- values: bfloat16 [32768, 4096], P('ctx', 'dp'), may hold values from -6 to 6
- cotangent: bfloat16 [32768, 4096], P('ctx', 'dp'), may hold values from -6 to 6
- log_decay: float32 [32], P('dp'), may hold values from 6.1035156e-06 to 0.04
- gain: float32 [4096], P(('dp', 'ctx')), may hold values from 0.1 to 1.9
Outputs:
- normed: bfloat16 [32768, 4096], P('ctx', 'dp')
- grad_queries: bfloat16 [32768, 4096], P('ctx', 'dp')
- grad_keys: bfloat16 [32768, 4096], P('ctx', 'dp')
- grad_values: bfloat16 [32768, 4096], P('ctx', 'dp')
- grad_gain: float32 [4096], P(('dp', 'ctx'))
All inputs are finite; a program needn't handle non-finite values.
Results may differ from a plain program's by a relative error of at most 0.0065.
Values may be sent and summed in bfloat16 or wider, within the bound.
A program may use at most 128 MiB of HBM per device.

v0:
```python
import jax
import jax.numpy as jnp
from jax import lax
from jax.sharding import PartitionSpec as P

HEAD = 128
HEADS = 32


eps_norm = 1e-06


def passed_along(value, axis, steps):
    count = lax.axis_size(axis)
    initial, last = (max(0, -steps), min(count, count - steps))
    return lax.ppermute(value, axis, [(source, source + steps) for source in range(initial, last)])


def decay_tables(log_decay, length):
    places = jnp.arange(length, dtype=jnp.float32)
    offsets = places[:, None] - places[None, :]
    rates = log_decay[:, None, None]
    decay_mask = jnp.where(
        offsets[None] >= 0.0, jnp.exp(-rates * jnp.maximum(offsets, 0.0)[None]), 0.0
    )
    from_start = jnp.exp(-log_decay[None, :] * (places[:, None] + 1.0))
    into_block = jnp.exp(-log_decay[None, :] * (length - 1.0 - places[:, None]))
    back_weight = jnp.exp(-log_decay[None, :] * places[:, None])
    back_rest = jnp.exp(-log_decay[None, :] * (length - places[:, None]))
    return (
        decay_mask,
        from_start[:, :, None],
        into_block[:, :, None],
        back_weight[:, :, None],
        back_rest[:, :, None],
    )


def combine_states(earlier, later):
    first_log, first_state = earlier
    second_log, second_state = later
    return (
        first_log + second_log,
        jnp.exp(-second_log)[:, None, None] * first_state + second_state,
    )


def carry_states(log_totals, states, backward):
    devices = lax.axis_size("ctx")
    direction = -1 if backward else 1
    distance = 1
    current = (log_totals, states)
    while distance < devices:
        arrived = passed_along((current[0], current[1]), "ctx", direction * distance)
        current = combine_states(arrived, current)
        distance = distance * 2
    return passed_along(current[1].astype(jnp.bfloat16), "ctx", direction)


def per_device(queries, keys, values, cotangent, log_decay, gain):
    length = queries.shape[0]
    heads = log_decay.shape[0]
    width = queries.shape[1] // heads
    channels = HEADS * HEAD
    shape = (length, heads, width)
    query_loc = queries.reshape(shape)
    key_loc = keys.reshape(shape)
    value_loc = values.reshape(shape)
    full_gain = lax.all_gather(gain, "ctx", axis=0, tiled=True).reshape(heads, width)
    decay_mask, from_start, into_block, back_weight, back_rest = decay_tables(log_decay, length)
    log_totals = log_decay * length
    key_weighted = (key_loc.astype(jnp.float32) * into_block).astype(jnp.bfloat16)
    block_state = jnp.einsum(
        "thd,the->hde", key_weighted, value_loc, preferred_element_type=jnp.float32
    )
    incoming_b = carry_states(log_totals, block_state, False)
    scores = jnp.einsum("thd,ihd->hti", query_loc, key_loc, preferred_element_type=jnp.float32)
    probs = (scores * decay_mask).astype(jnp.bfloat16)
    local_out = jnp.einsum("hti,ihe->the", probs, value_loc, preferred_element_type=jnp.float32)
    remote = jnp.einsum("thd,hde->the", query_loc, incoming_b, preferred_element_type=jnp.float32)
    attn = local_out + from_start * remote
    cot = cotangent.reshape(shape).astype(jnp.float32)
    square_part = jnp.sum(attn * attn, axis=(1, 2))
    cross_part = jnp.sum(cot * full_gain * attn, axis=(1, 2))
    square_total, cross_total = lax.psum((square_part, cross_part), "dp")
    inverse = lax.rsqrt(square_total / channels + eps_norm)[:, None, None]
    cross = cross_total[:, None, None]
    normed = (attn * inverse * full_gain).astype(jnp.bfloat16)
    grad_attn = (cot * full_gain * inverse - attn * inverse**3 * cross / channels).astype(
        jnp.bfloat16
    )
    gain_term = jnp.sum(cot * attn * inverse, axis=0).reshape(-1)
    grad_gain = lax.psum_scatter(gain_term, "ctx", scatter_dimension=0, tiled=True)
    query_weighted = (query_loc.astype(jnp.float32) * back_weight).astype(jnp.bfloat16)
    back_state = jnp.einsum(
        "thd,the->hde", query_weighted, grad_attn, preferred_element_type=jnp.float32
    )
    later_b = carry_states(log_totals, back_state, True)
    dscore = (
        jnp.einsum("the,ihe->hti", grad_attn, value_loc, preferred_element_type=jnp.float32)
        * decay_mask
    ).astype(jnp.bfloat16)
    grad_q = jnp.einsum("hti,ihd->thd", dscore, key_loc, preferred_element_type=jnp.float32)
    grad_q = grad_q + from_start * jnp.einsum(
        "the,hde->thd", grad_attn, incoming_b, preferred_element_type=jnp.float32
    )
    grad_k = jnp.einsum("hti,thd->ihd", dscore, query_loc, preferred_element_type=jnp.float32)
    grad_k = grad_k + back_rest * jnp.einsum(
        "ihe,hde->ihd", value_loc, later_b, preferred_element_type=jnp.float32
    )
    grad_v = jnp.einsum("hti,the->ihe", probs, grad_attn, preferred_element_type=jnp.float32)
    grad_v = grad_v + back_rest * jnp.einsum(
        "ihd,hde->ihe", key_loc, later_b, preferred_element_type=jnp.float32
    )
    flat = (length, heads * width)
    return (
        normed.reshape(flat),
        grad_q.astype(jnp.bfloat16).reshape(flat),
        grad_k.astype(jnp.bfloat16).reshape(flat),
        grad_v.astype(jnp.bfloat16).reshape(flat),
        grad_gain,
    )


def solution(mesh):
    in_specs = (
        P("ctx", "dp"),
        P("ctx", "dp"),
        P("ctx", "dp"),
        P("ctx", "dp"),
        P("dp"),
        P(("dp", "ctx")),
    )
    out_specs = (P("ctx", "dp"), P("ctx", "dp"), P("ctx", "dp"), P("ctx", "dp"), P(("dp", "ctx")))
    return jax.shard_map(
        per_device, mesh=mesh, in_specs=in_specs, out_specs=out_specs, check_vma=False
    )
```

profile of v0, /device:TPU:32, one launch (start us, length us, event | category | flops | bytes accessed | tf_op | source)
XLA Modules:
  0.0 581.0 jit_solution(17837068423072963668)
XLA Ops:
  1.4 7.4 %collective-permute-start.12 = (f32[4]{0:T(128)S(1)}, f32[4]{0:T(128)S(1)}, u32[]{:S(2)}, u32[]{:S(2)}) collective-permute-start(f32[4]{0:T(128)S(1)} %broadcast_multiply_fusion), channel_id=1, source_target_pairs={{8,0},{16,8},{24,16},{32,24},{40,32},{48,40},{56,48},{64,56},{72,6... | collective-permute-start | bytes 56 | tf_op jit(solution)/shard_map/ppermute | solution.py:16
  8.7 1.9 collective-permute-start
  12.0 2.2 collective-permute-done
  15.2 1.9 collective-permute-start.5
  17.2 6.3 %collective-permute-done.5 = f32[4,128,128]{2,1,0:T(8,128)S(1)} collective-permute-done((f32[4,128,128]{2,1,0:T(8,128)S(1)}, f32[4,128,128]{2,1,0:T(8,128)S(1)}, u32[]{:S(2)}, u32[]{:S(2)}) %collective-permute-start.5) | collective-permute-done | bytes 262176 | tf_op jit(solution)/shard_map/ppermute | solution.py:16
  23.6 2.2 collective-permute-start.6
  25.9 8.3 %collective-permute-done.6 = f32[4,128,128]{2,1,0:T(8,128)S(1)} collective-permute-done((f32[4,128,128]{2,1,0:T(8,128)S(1)}, f32[4,128,128]{2,1,0:T(8,128)S(1)}, u32[]{:S(2)}, u32[]{:S(2)}) %collective-permute-start.6) | collective-permute-done | bytes 262176 | tf_op jit(solution)/shard_map/ppermute | solution.py:16
  34.2 10.7 %collective-permute-start.7 = (f32[4,128,128]{2,1,0:T(8,128)S(1)}, f32[4,128,128]{2,1,0:T(8,128)S(1)}, u32[]{:S(2)}, u32[]{:S(2)}) collective-permute-start(f32[4,128,128]{2,1,0:T(8,128)S(1)} %multiply_add_fusion.8), channel_id=1, source_target_pairs={{0,32},{8,40},{16,48},{24,56},{32,64},{40,72},{48,80},{56,88},{64,... | collective-permute-start | bytes 786440 | tf_op jit(solution)/shard_map/ppermute | solution.py:16
  44.9 5.4 collective-permute-start.1
  50.3 6.0 %collective-permute-done.1 = f32[4]{0:T(128)S(1)} collective-permute-done((f32[4]{0:T(128)S(1)}, f32[4]{0:T(128)S(1)}, u32[]{:S(2)}, u32[]{:S(2)}) %collective-permute-start.1) | collective-permute-done | bytes 48 | tf_op jit(solution)/shard_map/ppermute | solution.py:16
  56.5 11.0 %collective-permute-start.8 = (f32[4,128,128]{2,1,0:T(8,128)S(1)}, f32[4,128,128]{2,1,0:T(8,128)S(1)}, u32[]{:S(2)}, u32[]{:S(2)}) collective-permute-start(f32[4,128,128]{2,1,0:T(8,128)S(1)} %multiply_add_fusion.7), channel_id=1, source_target_pairs={{0,64},{8,72},{16,80},{24,88},{32,96},{40,104},{48,112},{56,120},{... | collective-permute-start | bytes 786440 | tf_op jit(solution)/shard_map/ppermute | solution.py:16
  68.7 6.9 %collective-permute-start.2 = (f32[4]{0:T(128)S(1)}, f32[4]{0:T(128)S(1)}, u32[]{:S(2)}, u32[]{:S(2)}) collective-permute-start(f32[4]{0:T(128)S(1)} %get-tuple-element.30), channel_id=1, source_target_pairs={{0,32},{8,40},{16,48},{24,56},{32,64},{40,72},{48,80},{56,88},{64,... | collective-permute-start | bytes 56 | tf_op jit(solution)/shard_map/ppermute | solution.py:16
  75.6 1.3 collective-permute-done.2
  76.9 6.4 %collective-permute-done.8 = f32[4,128,128]{2,1,0:T(8,128)S(1)} collective-permute-done((f32[4,128,128]{2,1,0:T(8,128)S(1)}, f32[4,128,128]{2,1,0:T(8,128)S(1)}, u32[]{:S(2)}, u32[]{:S(2)}) %collective-permute-start.8) | collective-permute-done | bytes 262176 | tf_op jit(solution)/shard_map/ppermute | solution.py:16
  83.3 10.8 %collective-permute-start.9 = (f32[4,128,128]{2,1,0:T(8,128)S(1)}, f32[4,128,128]{2,1,0:T(8,128)}, u32[]{:S(2)}, u32[]{:S(2)}) collective-permute-start(f32[4,128,128]{2,1,0:T(8,128)S(1)} %multiply_add_fusion.6), channel_id=1, source_target_pairs={{0,128},{8,136},{16,144},{24,152},{32,160},{40,168},{48,176},{56,1... | collective-permute-start | bytes 786440 | tf_op jit(solution)/shard_map/ppermute | solution.py:16
  97.7 153.4 %all-reduce = f32[512]{0:T(512)S(1)} all-reduce(f32[512]{0:T(512)S(1)} %dynamic-update-slice), channel_id=1, replica_groups=mesh['ctx'=64,'dp'=8] {'ctx'}, use_global_device_ids=true, to_apply=%add | all-reduce | flops 512 | bytes 4096
  251.1 1.3 collective-permute-start.13
  252.4 1.3 collective-permute-start.3
  256.0 1.3 collective-permute-start.10
  257.3 2.6 multiply_convert_fusion.1
  260.0 2.9 collective-permute-start.4
  262.9 1.3 collective-permute-done.4
  264.3 2.7 collective-permute-start.11
  267.8 3.3 collective-permute-done.11
  271.5 12.8 %psum.14 = f32[512]{0:T(512)S(1)} all-reduce(f32[512]{0:T(512)S(1)} %get-tuple-element.47), channel_id=1, replica_groups=mesh['ctx'=64,'dp'=8] {'dp'}, use_global_device_ids=true, to_apply=%region_1.2 | all-reduce | flops 512 | bytes 4096 | tf_op jit(solution)/shard_map/psum | solution.py:85
  285.2 12.8 %psum.15 = f32[512]{0:T(512)S(1)} all-reduce(f32[512]{0:T(512)S(1)} %get-tuple-element.16), channel_id=1, replica_groups=mesh['ctx'=64,'dp'=8] {'dp'}, use_global_device_ids=true, to_apply=%region_3.4 | all-reduce | flops 512 | bytes 4096 | tf_op jit(solution)/shard_map/psum | solution.py:85
  299.4 2.1 collective-permute-start.17
  301.5 1.3 collective-permute-start.14
  302.8 12.0 %collective-permute-done.14 = f32[4]{0:T(128)S(1)} collective-permute-done((f32[4]{0:T(128)S(1)}, f32[4]{0:T(128)S(1)}, u32[]{:S(2)}, u32[]{:S(2)}) %collective-permute-start.14) | collective-permute-done | bytes 48 | tf_op jit(solution)/shard_map/ppermute | solution.py:16
  314.8 1.3 collective-permute-start.15
  316.2 1.3 collective-permute-start.18
  317.5 11.8 %collective-permute-done.15 = f32[4]{0:T(128)S(1)} collective-permute-done((f32[4]{0:T(128)S(1)}, f32[4]{0:T(128)S(1)}, u32[]{:S(2)}, u32[]{:S(2)}) %collective-permute-start.15) | collective-permute-done | bytes 48 | tf_op jit(solution)/shard_map/ppermute | solution.py:16
  329.3 1.3 collective-permute-start.16
  330.6 12.1 %collective-permute-done.16 = f32[4]{0:T(128)S(1)} collective-permute-done((f32[4]{0:T(128)S(1)}, f32[4]{0:T(128)S(1)}, u32[]{:S(2)}, u32[]{:S(2)}) %collective-permute-start.16) | collective-permute-done | bytes 48 | tf_op jit(solution)/shard_map/ppermute | solution.py:16
  342.8 1.4 collective-permute-start.19
  344.2 1.4 multiply_convert_fusion
  345.7 15.1 %collective-permute-done.19 = f32[4,128,128]{2,1,0:T(8,128)S(1)} collective-permute-done((f32[4,128,128]{2,1,0:T(8,128)S(1)}, f32[4,128,128]{2,1,0:T(8,128)S(1)}, u32[]{:S(2)}, u32[]{:S(2)}) %collective-permute-start.19) | collective-permute-done | bytes 262176 | tf_op jit(solution)/shard_map/ppermute | solution.py:16
  360.9 1.3 collective-permute-start.20
  362.7 33.2 %collective-permute-done.20 = f32[4,128,128]{2,1,0:T(8,128)S(1)} collective-permute-done((f32[4,128,128]{2,1,0:T(8,128)S(1)}, f32[4,128,128]{2,1,0:T(8,128)S(1)}, u32[]{:S(2)}, u32[]{:S(2)}) %collective-permute-start.20) | collective-permute-done | bytes 262176 | tf_op jit(solution)/shard_map/ppermute | solution.py:16
  395.9 1.4 collective-permute-start.21
  397.8 7.4 %collective-permute-done.21 = f32[4,128,128]{2,1,0:T(8,128)S(1)} collective-permute-done((f32[4,128,128]{2,1,0:T(8,128)S(1)}, f32[4,128,128]{2,1,0:T(8,128)S(1)}, u32[]{:S(2)}, u32[]{:S(2)}) %collective-permute-start.21) | collective-permute-done | bytes 262176 | tf_op jit(solution)/shard_map/ppermute | solution.py:16
  405.3 1.3 collective-permute-start.22
  407.4 12.3 %collective-permute-done.22 = f32[4,128,128]{2,1,0:T(8,128)S(1)} collective-permute-done((f32[4,128,128]{2,1,0:T(8,128)S(1)}, f32[4,128,128]{2,1,0:T(8,128)S(1)}, u32[]{:S(2)}, u32[]{:S(2)}) %collective-permute-start.22) | collective-permute-done | bytes 262176 | tf_op jit(solution)/shard_map/ppermute | solution.py:16
  419.8 13.6 %collective-permute-start.23 = (bf16[4,128,128]{2,1,0:T(8,128)(2,1)S(1)}, bf16[4,128,128]{2,1,0:T(8,128)(2,1)S(1)}, u32[]{:S(2)}, u32[]{:S(2)}) collective-permute-start(bf16[4,128,128]{2,1,0:T(8,128)(2,1)S(1)} %add_convert_fusion), channel_id=1, source_target_pairs={{8,0},{16,8},{24,16},{32,24},{40,32},{48,40},{56,48},{64,56},{72,6... | collective-permute-start | bytes 393224 | tf_op jit(solution)/shard_map/ppermute | solution.py:16
  434.5 2.0 copy.51
  436.6 2.0 copy.52
  438.6 137.3 %all-reduce.1 = f32[512]{0:T(512)S(1)} all-reduce(f32[512]{0:T(512)} %bitcast.114), channel_id=2, replica_groups=mesh['ctx'=64,'dp'=8] {'ctx'}, use_global_device_ids=true, to_apply=%region_5.6.clone | all-reduce | flops 512 | bytes 4096
  577.7 2.0 copy.54
  (83 shorter events, 19.3 us)
Async XLA Ops:
  0.6 14.3 %copy-start = (bf16[512,512]{1,0:T(8,128)(2,1)S(1)}, bf16[512,512]{1,0:T(8,128)(2,1)}, u32[]{:S(2)}) copy-start(bf16[512,512]{1,0:T(8,128)(2,1)} %param.8) | copy-start | bytes 1572868
  1.4 10.6 %collective-permute-start.12 = (f32[4]{0:T(128)S(1)}, f32[4]{0:T(128)S(1)}, u32[]{:S(2)}, u32[]{:S(2)}) collective-permute-start(f32[4]{0:T(128)S(1)} %broadcast_multiply_fusion), channel_id=1, source_target_pairs={{8,0},{16,8},{24,16},{32,24},{40,32},{48,40},{56,48},{64,56},{72,6... | collective-permute-start | bytes 56 | tf_op jit(solution)/shard_map/ppermute | solution.py:16
  8.7 5.4 collective-permute-start
  12.0 56.7 %copy-start.5 = (bf16[512,512]{0,1:T(8,128)(2,1)}, bf16[512,512]{0,1:T(8,128)(2,1)S(1)}, u32[]{:S(2)}) copy-start(bf16[512,512]{0,1:T(8,128)(2,1)S(1)} %copy.87) | copy-start | bytes 1572868
  15.2 8.3 %collective-permute-start.5 = (f32[4,128,128]{2,1,0:T(8,128)S(1)}, f32[4,128,128]{2,1,0:T(8,128)S(1)}, u32[]{:S(2)}, u32[]{:S(2)}) collective-permute-start(f32[4,128,128]{2,1,0:T(8,128)S(1)} %fusion.13), channel_id=1, source_target_pairs={{0,8},{8,16},{16,24},{24,32},{32,40},{40,48},{48,56},{56,64},{64,7... | collective-permute-start | bytes 786440 | tf_op jit(solution)/shard_map/ppermute | solution.py:16
  23.5 71.5 %copy-start.9 = (bf16[512,512]{1,0:T(8,128)(2,1)S(1)}, bf16[512,512]{1,0:T(8,128)(2,1)}, u32[]{:S(2)}) copy-start(bf16[512,512]{1,0:T(8,128)(2,1)} %param.6) | copy-start | bytes 1572868
  23.6 10.5 %collective-permute-start.6 = (f32[4,128,128]{2,1,0:T(8,128)S(1)}, f32[4,128,128]{2,1,0:T(8,128)S(1)}, u32[]{:S(2)}, u32[]{:S(2)}) collective-permute-start(f32[4,128,128]{2,1,0:T(8,128)S(1)} %multiply_add_fusion.9), channel_id=1, source_target_pairs={{0,16},{8,24},{16,32},{24,40},{32,48},{40,56},{48,64},{56,72},{64,... | collective-permute-start | bytes 786440 | tf_op jit(solution)/shard_map/ppermute | solution.py:16
  34.2 61.0 %copy-start.8 = (bf16[512,512]{1,0:T(8,128)(2,1)S(1)}, bf16[512,512]{1,0:T(8,128)(2,1)}, u32[]{:S(2)}) copy-start(bf16[512,512]{1,0:T(8,128)(2,1)} %param.9) | copy-start | bytes 1572868
  34.2 22.1 %collective-permute-start.7 = (f32[4,128,128]{2,1,0:T(8,128)S(1)}, f32[4,128,128]{2,1,0:T(8,128)S(1)}, u32[]{:S(2)}, u32[]{:S(2)}) collective-permute-start(f32[4,128,128]{2,1,0:T(8,128)S(1)} %multiply_add_fusion.8), channel_id=1, source_target_pairs={{0,32},{8,40},{16,48},{24,56},{32,64},{40,72},{48,80},{56,88},{64,... | collective-permute-start | bytes 786440 | tf_op jit(solution)/shard_map/ppermute | solution.py:16
  44.9 11.4 %collective-permute-start.1 = (f32[4]{0:T(128)S(1)}, f32[4]{0:T(128)S(1)}, u32[]{:S(2)}, u32[]{:S(2)}) collective-permute-start(f32[4]{0:T(128)S(1)} %get-tuple-element.44), channel_id=1, source_target_pairs={{0,16},{8,24},{16,32},{24,40},{32,48},{40,56},{48,64},{56,72},{64,... | collective-permute-start | bytes 56 | tf_op jit(solution)/shard_map/ppermute | solution.py:16
  56.5 26.8 %collective-permute-start.8 = (f32[4,128,128]{2,1,0:T(8,128)S(1)}, f32[4,128,128]{2,1,0:T(8,128)S(1)}, u32[]{:S(2)}, u32[]{:S(2)}) collective-permute-start(f32[4,128,128]{2,1,0:T(8,128)S(1)} %multiply_add_fusion.7), channel_id=1, source_target_pairs={{0,64},{8,72},{16,80},{24,88},{32,96},{40,104},{48,112},{56,120},{... | collective-permute-start | bytes 786440 | tf_op jit(solution)/shard_map/ppermute | solution.py:16
  68.7 26.8 %copy-start.11 = (u32[512]{0:T(512)S(1)}, u32[512]{0:T(512)}, u32[]{:S(2)}) copy-start(u32[512]{0:T(512)} %constant.22) | copy-start | bytes 6148
  68.7 28.8 %copy-start.12 = (f32[8]{0:T(128)S(1)}, f32[8]{0:T(128)}, u32[]{:S(2)}) copy-start(f32[8]{0:T(128)} %param.11) | copy-start | bytes 100
  68.7 8.2 %collective-permute-start.2 = (f32[4]{0:T(128)S(1)}, f32[4]{0:T(128)S(1)}, u32[]{:S(2)}, u32[]{:S(2)}) collective-permute-start(f32[4]{0:T(128)S(1)} %get-tuple-element.30), channel_id=1, source_target_pairs={{0,32},{8,40},{16,48},{24,56},{32,64},{40,72},{48,80},{56,88},{64,... | collective-permute-start | bytes 56 | tf_op jit(solution)/shard_map/ppermute | solution.py:16
  83.2 174.1 %copy-start.3 = (bf16[512,512]{1,0:T(8,128)(2,1)S(1)}, bf16[512,512]{1,0:T(8,128)(2,1)}, u32[]{:S(2)}) copy-start(bf16[512,512]{1,0:T(8,128)(2,1)} %param.7) | copy-start | bytes 1572868
  83.3 171.6 %collective-permute-start.9 = (f32[4,128,128]{2,1,0:T(8,128)S(1)}, f32[4,128,128]{2,1,0:T(8,128)}, u32[]{:S(2)}, u32[]{:S(2)}) collective-permute-start(f32[4,128,128]{2,1,0:T(8,128)S(1)} %multiply_add_fusion.6), channel_id=1, source_target_pairs={{0,128},{8,136},{16,144},{24,152},{32,160},{40,168},{48,176},{56,1... | collective-permute-start | bytes 786440 | tf_op jit(solution)/shard_map/ppermute | solution.py:16
  251.1 50.4 %collective-permute-start.13 = (f32[4]{0:T(128)S(1)}, f32[4]{0:T(128)S(1)}, u32[]{:S(2)}, u32[]{:S(2)}) collective-permute-start(f32[4]{0:T(128)S(1)} %get-tuple-element.24), channel_id=1, source_target_pairs={{16,0},{24,8},{32,16},{40,24},{48,32},{56,40},{64,48},{72,56},{80,... | collective-permute-start | bytes 56 | tf_op jit(solution)/shard_map/ppermute | solution.py:16
  252.4 2.6 collective-permute-start.3
  256.0 8.1 %collective-permute-start.10 = (f32[4,128,128]{2,1,0:T(8,128)S(1)}, f32[4,128,128]{2,1,0:T(8,128)S(1)}, u32[]{:S(2)}, u32[]{:S(2)}) collective-permute-start(f32[4,128,128]{2,1,0:T(8,128)S(1)} %multiply_add_fusion.5), channel_id=1, source_target_pairs={{0,256},{8,264},{16,272},{24,280},{32,288},{40,296},{48,304},{56,3... | collective-permute-start | bytes 786440 | tf_op jit(solution)/shard_map/ppermute | solution.py:16
  260.0 7.8 %copy-start.1 = (bf16[4,512,512]{2,1,0:T(8,128)(2,1)}, bf16[4,512,512]{2,1,0:T(8,128)(2,1)S(1)}, u32[]{:S(2)}) copy-start(bf16[4,512,512]{2,1,0:T(8,128)(2,1)S(1)} %multiply_convert_fusion.1) | copy-start | bytes 6291460
  260.0 4.1 collective-permute-start.4
  264.3 6.9 %collective-permute-start.11 = (bf16[4,128,128]{2,1,0:T(8,128)(2,1)S(1)}, bf16[4,128,128]{2,1,0:T(8,128)(2,1)S(1)}, u32[]{:S(2)}, u32[]{:S(2)}) collective-permute-start(bf16[4,128,128]{2,1,0:T(8,128)(2,1)S(1)} %add_convert_fusion.1), channel_id=1, source_target_pairs={{0,8},{8,16},{16,24},{24,32},{32,40},{40,48},{48,56},{56,64},{64,7... | collective-permute-start | bytes 393224 | tf_op jit(solution)/shard_map/ppermute | solution.py:16
  299.1 45.1 %copy-start.7 = (f32[512,512]{1,0:T(8,128)S(1)}, f32[512,512]{1,0:T(8,128)}, u32[]{:S(2)}) copy-start(f32[512,512]{1,0:T(8,128)} %fusion.11) | copy-start | bytes 3145732
  299.1 45.1 %copy-start.10 = (pred[512,512]{1,0:T(8,128)(4,1)S(1)}, pred[512,512]{1,0:T(8,128)(4,1)}, u32[]{:S(2)}) copy-start(pred[512,512]{1,0:T(8,128)(4,1)} %fusion.12) | copy-start | bytes 786436
  299.4 16.6 %collective-permute-start.17 = (f32[4,128,128]{2,1,0:T(8,128)S(1)}, f32[4,128,128]{2,1,0:T(8,128)S(1)}, u32[]{:S(2)}, u32[]{:S(2)}) collective-permute-start(f32[4,128,128]{2,1,0:T(8,128)S(1)} %fusion.14), channel_id=1, source_target_pairs={{8,0},{16,8},{24,16},{32,24},{40,32},{48,40},{56,48},{64,56},{72,6... | collective-permute-start | bytes 786440 | tf_op jit(solution)/shard_map/ppermute | solution.py:16
  301.5 13.3 %collective-permute-start.14 = (f32[4]{0:T(128)S(1)}, f32[4]{0:T(128)S(1)}, u32[]{:S(2)}, u32[]{:S(2)}) collective-permute-start(f32[4]{0:T(128)S(1)} %get-tuple-element.22), channel_id=1, source_target_pairs={{32,0},{40,8},{48,16},{56,24},{64,32},{72,40},{80,48},{88,56},{96,... | collective-permute-start | bytes 56 | tf_op jit(solution)/shard_map/ppermute | solution.py:16
  314.8 14.5 %collective-permute-start.15 = (f32[4]{0:T(128)S(1)}, f32[4]{0:T(128)S(1)}, u32[]{:S(2)}, u32[]{:S(2)}) collective-permute-start(f32[4]{0:T(128)S(1)} %get-tuple-element.20), channel_id=1, source_target_pairs={{64,0},{72,8},{80,16},{88,24},{96,32},{104,40},{112,48},{120,56},{... | collective-permute-start | bytes 56 | tf_op jit(solution)/shard_map/ppermute | solution.py:16
  316.2 26.5 %collective-permute-start.18 = (f32[4,128,128]{2,1,0:T(8,128)S(1)}, f32[4,128,128]{2,1,0:T(8,128)S(1)}, u32[]{:S(2)}, u32[]{:S(2)}) collective-permute-start(f32[4,128,128]{2,1,0:T(8,128)S(1)} %multiply_add_fusion.4), channel_id=1, source_target_pairs={{16,0},{24,8},{32,16},{40,24},{48,32},{56,40},{64,48},{72,56},{80,... | collective-permute-start | bytes 786440 | tf_op jit(solution)/shard_map/ppermute | solution.py:16
  329.3 13.4 %collective-permute-start.16 = (f32[4]{0:T(128)S(1)}, f32[4]{0:T(128)S(1)}, u32[]{:S(2)}, u32[]{:S(2)}) collective-permute-start(f32[4]{0:T(128)S(1)} %get-tuple-element.18), channel_id=1, source_target_pairs={{128,0},{136,8},{144,16},{152,24},{160,32},{168,40},{176,48},{184,... | collective-permute-start | bytes 56 | tf_op jit(solution)/shard_map/ppermute | solution.py:16
  342.8 19.4 %copy-start.2 = (bf16[4,512,512]{2,1,0:T(8,128)(2,1)S(1)}, bf16[4,512,512]{2,1,0:T(8,128)(2,1)}, u32[]{:S(2)}) copy-start(bf16[4,512,512]{2,1,0:T(8,128)(2,1)} %copy-done.1) | copy-start | bytes 6291460
  342.8 18.0 %collective-permute-start.19 = (f32[4,128,128]{2,1,0:T(8,128)S(1)}, f32[4,128,128]{2,1,0:T(8,128)S(1)}, u32[]{:S(2)}, u32[]{:S(2)}) collective-permute-start(f32[4,128,128]{2,1,0:T(8,128)S(1)} %multiply_add_fusion.3), channel_id=1, source_target_pairs={{32,0},{40,8},{48,16},{56,24},{64,32},{72,40},{80,48},{88,56},{96,... | collective-permute-start | bytes 786440 | tf_op jit(solution)/shard_map/ppermute | solution.py:16
  360.9 34.9 %collective-permute-start.20 = (f32[4,128,128]{2,1,0:T(8,128)S(1)}, f32[4,128,128]{2,1,0:T(8,128)S(1)}, u32[]{:S(2)}, u32[]{:S(2)}) collective-permute-start(f32[4,128,128]{2,1,0:T(8,128)S(1)} %multiply_add_fusion.2), channel_id=1, source_target_pairs={{64,0},{72,8},{80,16},{88,24},{96,32},{104,40},{112,48},{120,56},{... | collective-permute-start | bytes 786440 | tf_op jit(solution)/shard_map/ppermute | solution.py:16
  395.9 10.7 %copy-start.6 = (bf16[512,512]{0,1:T(8,128)(2,1)S(1)}, bf16[512,512]{0,1:T(8,128)(2,1)}, u32[]{:S(2)}) copy-start(bf16[512,512]{0,1:T(8,128)(2,1)} %copy-done.5) | copy-start | bytes 1572868
  395.9 9.3 %collective-permute-start.21 = (f32[4,128,128]{2,1,0:T(8,128)S(1)}, f32[4,128,128]{2,1,0:T(8,128)S(1)}, u32[]{:S(2)}, u32[]{:S(2)}) collective-permute-start(f32[4,128,128]{2,1,0:T(8,128)S(1)} %multiply_add_fusion.1), channel_id=1, source_target_pairs={{128,0},{136,8},{144,16},{152,24},{160,32},{168,40},{176,48},{184,... | collective-permute-start | bytes 786440 | tf_op jit(solution)/shard_map/ppermute | solution.py:16
  405.3 14.4 %collective-permute-start.22 = (f32[4,128,128]{2,1,0:T(8,128)S(1)}, f32[4,128,128]{2,1,0:T(8,128)S(1)}, u32[]{:S(2)}, u32[]{:S(2)}) collective-permute-start(f32[4,128,128]{2,1,0:T(8,128)S(1)} %multiply_add_fusion), channel_id=1, source_target_pairs={{256,0},{264,8},{272,16},{280,24},{288,32},{296,40},{304,48},{312,... | collective-permute-start | bytes 786440 | tf_op jit(solution)/shard_map/ppermute | solution.py:16
  419.8 156.7 %copy-start.4 = (bf16[512,512]{1,0:T(8,128)(2,1)S(1)}, bf16[512,512]{1,0:T(8,128)(2,1)}, u32[]{:S(2)}) copy-start(bf16[512,512]{1,0:T(8,128)(2,1)} %param.7) | copy-start | bytes 1572868
  419.8 156.7 %collective-permute-start.23 = (bf16[4,128,128]{2,1,0:T(8,128)(2,1)S(1)}, bf16[4,128,128]{2,1,0:T(8,128)(2,1)S(1)}, u32[]{:S(2)}, u32[]{:S(2)}) collective-permute-start(bf16[4,128,128]{2,1,0:T(8,128)(2,1)S(1)} %add_convert_fusion), channel_id=1, source_target_pairs={{8,0},{16,8},{24,16},{32,24},{40,32},{48,40},{56,48},{64,56},{72,6... | collective-permute-start | bytes 393224 | tf_op jit(solution)/shard_map/ppermute | solution.py:16
where the time goes:
time: 582 us; the launch traced here: 581 us
  blocking collectives  316 us (54%)
  waiting for transfers between devices  140 us (24%)
  starting transfers between devices  93.9 us (16%)
  local copies, waits for them, and re-layouts  10.3 us (2%)
  matrix products  10 us (2%)
  other arithmetic  7.8 us (1%)
    unnamed x2, blocking collectives  291 us
    ppermute x24, waiting for transfers between devices, passed_along(): lax.ppermute(value, axis, [(source, source + steps) for source in range(i...  140 us
    ppermute x24, starting transfers between devices, passed_along(): lax.ppermute(value, axis, [(source, source + steps) for source in range(i...  93.9 us
    psum x2, blocking collectives, per_device(): square_total, cross_total = lax.psum((square_part, cross_part), 'dp')  25.5 us
  transfers between devices with their start and end apart: 24, of which 16 were waited for; matrix products, arithmetic and copies ran while one was open for 4% of the time, Pallas kernels for 0%

commit v1 on v0

v1 whole, which is shorter than its diff:
```python
import functools

import jax
import jax.numpy as jnp
from jax import lax
from jax.experimental import pallas as pl
from jax.experimental.pallas import tpu as pltpu
from jax.sharding import PartitionSpec as P

HEAD = 128
LOCAL = 4
TOK = 512
WIDE = LOCAL * HEAD
SUB = 128
BLOCKS = TOK // SUB
HALF = 256
X = 4
PAIR = 2 * HEAD

eps_norm = 1e-06
F32, BF16 = jnp.float32, jnp.bfloat16
MESH = pl.DeviceIdType.MESH
HIGH = lax.Precision.HIGHEST


def dot(a, b, over_a, over_b, precision=None):
    return lax.dot_general(
        a, b, (((over_a,), (over_b,)), ((), ())), precision=precision, preferred_element_type=F32
    )


def each_peer(count, me, body):
    def step(i, carry):
        offset = count // 2 + ((i + 1) // 2) * (1 - 2 * lax.rem(i, 2))
        body(lax.rem(me + offset, count))
        return carry

    lax.fori_loop(0, count - 1, step, 0)


def wait_for(ref, sem):
    pltpu.make_async_copy(ref, ref, sem).wait()


class Scan:
    def __init__(self, place, rate_ref, backward, refs):
        self.x, self.z, self.Z = place
        self.rate_ref = rate_ref
        self.backward = backward
        self.send, self.gather, self.pre, self.totals, self.back, self.result, self.sems = refs
        self.rows = PAIR // self.Z

    def sem(self, kind, j):
        return self.sems.at[kind, j]

    def rate(self, j):
        return self.rate_ref[2 * j + self.z // (self.Z // 2)]

    def exchange(self, j):
        rows, z = self.rows, self.z

        def one(peer):
            pltpu.make_async_remote_copy(
                src_ref=self.send.at[pl.ds(pl.multiple_of(j * PAIR + peer * rows, rows), rows)],
                dst_ref=self.gather.at[j, z],
                send_sem=self.sem(0, j),
                recv_sem=self.sem(1, j),
                device_id={"ctx": self.x * self.Z + peer},
                device_id_type=MESH,
            ).start()

        each_peer(self.Z, z, one)
        own = self.send[pl.ds(pl.multiple_of(j * PAIR + z * rows, rows), rows)]
        self.gather[j, z] = own

    def total(self, j):
        rows, x = self.rows, self.x
        wait_for(self.gather.at[j, pl.ds(0, self.Z - 1)], self.sem(1, j))
        decay = jnp.exp(jnp.full((rows, HEAD), -float(TOK) * self.rate(j), F32))
        state = jnp.zeros((rows, HEAD), F32)
        order = range(self.Z - 1, -1, -1) if self.backward else range(self.Z)
        for place in order:
            self.pre[j, place] = state
            state = decay * state + self.gather[j, place].astype(F32)
        self.totals[j, x] = state

        def one(peer):
            pltpu.make_async_remote_copy(
                src_ref=self.totals.at[j, x],
                dst_ref=self.totals.at[j, x],
                send_sem=self.sem(2, j),
                recv_sem=self.sem(3, j),
                device_id={"ctx": peer * self.Z + self.z},
                device_id_type=MESH,
            ).start()

        each_peer(X, x, one)

    def finish(self, j):
        rows, x, z = self.rows, self.x, self.z
        wait_for(self.totals.at[j, pl.ds(0, X - 1)], self.sem(3, j))
        rate = self.rate(j)
        far = jnp.zeros((rows, HEAD), F32)
        for other in range(X):
            steps = (other - x - 1) if self.backward else (x - other - 1)
            reach = jnp.maximum(steps, 0).astype(F32) * (float(TOK) * self.Z)
            weight = jnp.exp(jnp.full((rows, HEAD), -reach * rate, F32))
            far = far + jnp.where(steps >= 0, weight * self.totals[j, other], 0.0)
        decay = jnp.exp(jnp.full((rows, HEAD), -float(TOK) * rate, F32))
        order = range(self.Z - 1, -1, -1) if self.backward else range(self.Z)
        for place in order:
            self.back[j, place] = (self.pre[j, place] + far).astype(BF16)
            far = far * decay

        def one(peer):
            pltpu.make_async_remote_copy(
                src_ref=self.back.at[j, peer],
                dst_ref=self.result.at[pl.ds(pl.multiple_of(j * PAIR + z * rows, rows), rows)],
                send_sem=self.sem(4, j),
                recv_sem=self.sem(5, j),
                device_id={"ctx": x * self.Z + peer},
                device_id_type=MESH,
            ).start()

        each_peer(self.Z, z, one)
        self.result[pl.ds(pl.multiple_of(j * PAIR + z * rows, rows), rows)] = self.back[j, z]

    def arrived(self, j):
        wait_for(self.back.at[j, pl.ds(0, self.Z - 1)], self.sem(5, j))

    def close(self):
        for j in range(2):
            wait_for(self.gather.at[j, pl.ds(0, self.Z - 1)], self.sem(0, j))
            wait_for(self.totals.at[j, pl.ds(0, X - 1)], self.sem(2, j))
            wait_for(self.back.at[j, pl.ds(0, self.Z - 1)], self.sem(4, j))


def kernel(
    Z,
    DP,
    rate_ref,
    gain_ref,
    q_hbm,
    k_hbm,
    v_hbm,
    cot_hbm,
    normed,
    gq,
    gk,
    gv,
    gg_ref,
    q,
    k,
    v,
    cot,
    grad,
    weighted,
    probs,
    dscore,
    mask,
    down_base,
    up_base,
    attn,
    gk_part,
    gv_part,
    norm_parts,
    gain_z,
    gain_x,
    term,
    term_x,
    term_z,
    *rest,
):
    forward_refs, backward_refs = rest[0:7], rest[7:14]
    load_sems, small_sems = rest[14:]
    ctx, d = lax.axis_index("ctx"), lax.axis_index("dp")
    x, z = ctx // Z, lax.rem(ctx, Z)
    channels = DP * WIDE
    share = WIDE // (X * Z)

    loads = [
        pltpu.make_async_copy(source, target, load_sems.at[i])
        for i, (source, target) in enumerate(
            ((k_hbm, k), (v_hbm, v), (q_hbm, q), (cot_hbm, cot))
        )
    ]
    for load in loads:
        load.start()

    barrier = pltpu.get_barrier_semaphore()

    def greet_row(peer):
        pl.semaphore_signal(
            barrier, inc=1, device_id={"ctx": x * Z + peer}, device_id_type=MESH
        )

    def greet_rows(peer):
        pl.semaphore_signal(
            barrier, inc=1, device_id={"ctx": peer * Z + z}, device_id_type=MESH
        )

    def greet_dp(peer):
        pl.semaphore_signal(barrier, inc=1, device_id={"dp": peer}, device_id_type=MESH)

    each_peer(Z, z, greet_row)
    each_peer(X, x, greet_rows)
    each_peer(DP, d, greet_dp)

    place = (x, z, Z)
    ahead = Scan(place, rate_ref, False, forward_refs)
    behind = Scan(place, rate_ref, True, backward_refs)
    incoming, later = ahead.result, behind.result

    def lanes(h):
        return slice(h * HEAD, (h + 1) * HEAD)

    def rows_of(b):
        return slice(b * SUB, (b + 1) * SUB)

    def scaled(h, count):
        return jnp.exp(jnp.full((1, HEAD), -float(count) * rate_ref[h], F32))

    row_index = lax.broadcasted_iota(jnp.int32, (SUB, HEAD), 0).astype(F32)

    def make_up(h):
        up_base[h] = jnp.exp(-rate_ref[h] * (SUB - 1.0 - row_index))

    def make_down(h):
        down_base[h] = jnp.exp(-rate_ref[h] * row_index)

    def up(h, b, extra=0):
        return up_base[h] * scaled(h, SUB * (BLOCKS - 1 - b) + extra)

    def down(h, b, extra=0):
        return down_base[h] * scaled(h, SUB * b + extra)

    def make_mask(h):
        t = lax.broadcasted_iota(jnp.int32, (HALF, HALF), 0)
        i = lax.broadcasted_iota(jnp.int32, (HALF, HALF), 1)
        offset = (t - i).astype(F32)
        near = jnp.exp(-rate_ref[h] * jnp.maximum(offset, 0.0))
        mask[h, 0] = jnp.where(t >= i, near, 0.0)
        mask[h, 1] = jnp.exp(-rate_ref[h] * (offset + float(HALF)))

    def block_state(h):
        make_up(h)
        weighted_k = jnp.concatenate(
            [
                (k[rows_of(b), lanes(h)].astype(F32) * up(h, b)).astype(BF16)
                for b in range(BLOCKS)
            ],
            axis=0,
        )
        state = dot(weighted_k, v[:, lanes(h)], 0, 0)
        ahead.send[pl.ds(h * HEAD, HEAD)] = state.astype(BF16)

    def masked(h, left, right, out):
        for tb in range(2):
            rows = slice(tb * HALF, (tb + 1) * HALF)
            for ib in range(tb + 1):
                cols = slice(ib * HALF, (ib + 1) * HALF)
                score = dot(left[rows, lanes(h)], right[cols, lanes(h)], 1, 1)
                out[h, rows, cols] = (score * mask[h, tb - ib]).astype(BF16)

    def below(table, h, right):
        return (
            dot(table[h, 0:HALF, 0:HALF], right[0:HALF, lanes(h)], 1, 0),
            dot(table[h, HALF:TOK, :], right[:, lanes(h)], 1, 0),
        )

    def above(table, h, right):
        return (
            dot(table[h, :, 0:HALF], right[:, lanes(h)], 0, 0),
            dot(table[h, HALF:TOK, HALF:TOK], right[HALF:TOK, lanes(h)], 0, 0),
        )

    def local_part(h):
        make_mask(h)
        masked(h, q, k, probs)
        first, second = below(probs, h, v)
        attn[0:HALF, lanes(h)] = first
        attn[HALF:TOK, lanes(h)] = second

    def weigh_queries(h):
        make_down(h)
        for b in range(BLOCKS):
            weighted[rows_of(b), lanes(h)] = (
                q[rows_of(b), lanes(h)].astype(F32) * down(h, b)
            ).astype(BF16)

    def add_remote(h):
        remote = dot(q[:, lanes(h)], incoming[pl.ds(h * HEAD, HEAD)], 1, 0)
        for b in range(BLOCKS):
            attn[rows_of(b), lanes(h)] += down(h, b, 1) * remote[rows_of(b)]

    def send_row(source, target, kind, peer_ctx):
        pltpu.make_async_remote_copy(
            src_ref=source,
            dst_ref=target,
            send_sem=small_sems.at[kind],
            recv_sem=small_sems.at[kind + 1],
            device_id={"ctx": peer_ctx},
            device_id_type=MESH,
        ).start()

    lane = lax.broadcasted_iota(jnp.int32, (1, HEAD), 1)

    def gather_gain():
        own = jnp.zeros((1, HEAD), F32)
        for n in range(share):
            own = jnp.where(lane == z * share + n, gain_ref[n], own)
        gain_z[z] = own
        each_peer(Z, z, lambda peer: send_row(gain_z.at[z], gain_z.at[z], 0, x * Z + peer))

    def spread_gain():
        wait_for(gain_z.at[pl.ds(0, Z - 1)], small_sems.at[1])
        whole = gain_z[0]
        for n in range(1, Z):
            whole = whole + gain_z[n]
        gain_x[x] = whole
        each_peer(X, x, lambda peer: send_row(gain_x.at[x], gain_x.at[x], 2, peer * Z + z))

    def gain_arrived():
        wait_for(gain_x.at[pl.ds(0, X - 1)], small_sems.at[3])

    loads[0].wait()
    loads[1].wait()
    block_state(0)
    block_state(1)
    pl.semaphore_wait(barrier, (Z - 1) + (X - 1) + (DP - 1))
    ahead.exchange(0)
    block_state(2)
    block_state(3)
    ahead.exchange(1)
    gather_gain()
    loads[2].wait()
    local_part(0)
    local_part(1)
    ahead.total(0)
    weigh_queries(0)
    weigh_queries(1)
    ahead.finish(0)
    ahead.total(1)
    spread_gain()
    local_part(2)
    ahead.finish(1)
    local_part(3)
    weigh_queries(2)
    weigh_queries(3)
    loads[3].wait()
    gain_arrived()
    ahead.arrived(0)
    add_remote(0)
    add_remote(1)
    ahead.arrived(1)
    add_remote(2)
    add_remote(3)

    ones = jnp.ones((8, HEAD), F32)
    row8 = lax.broadcasted_iota(jnp.int32, (8, HEAD), 0)
    sums = jnp.zeros((8, HEAD), F32)
    for b in range(BLOCKS):
        square = jnp.zeros((SUB, HEAD), F32)
        cross = jnp.zeros((SUB, HEAD), F32)
        for h in range(LOCAL):
            a = attn[rows_of(b), lanes(h)]
            square = square + a * a
            cross = cross + cot[rows_of(b), lanes(h)].astype(F32) * gain_x[h] * a
        sums = jnp.where(row8 == b, dot(ones, square, 1, 1, HIGH), sums)
        sums = jnp.where(row8 == b + BLOCKS, dot(ones, cross, 1, 1, HIGH), sums)
    norm_parts[d] = sums

    def send_norm(peer):
        pltpu.make_async_remote_copy(
            src_ref=norm_parts.at[d],
            dst_ref=norm_parts.at[d],
            send_sem=small_sems.at[4],
            recv_sem=small_sems.at[5],
            device_id={"dp": peer},
            device_id_type=MESH,
        ).start()

    each_peer(DP, d, send_norm)
    wait_for(norm_parts.at[pl.ds(0, DP - 1)], small_sems.at[5])
    whole = norm_parts[0]
    for n in range(1, DP):
        whole = whole + norm_parts[n]
    inverse_rows = lax.rsqrt(whole[0:BLOCKS] / channels + eps_norm)
    cross_rows = inverse_rows * inverse_rows * inverse_rows * whole[BLOCKS : 2 * BLOCKS] / channels

    def column(rows, b):
        return jnp.broadcast_to(rows[b : b + 1], (SUB, HEAD)).T

    inverse = [column(inverse_rows, b) for b in range(BLOCKS)]
    cross_part = [column(cross_rows, b) for b in range(BLOCKS)]

    def back_state(h):
        for b in range(BLOCKS):
            at = (rows_of(b), lanes(h))
            grad[at] = (
                cot[at].astype(F32) * gain_x[h] * inverse[b] - attn[at] * cross_part[b]
            ).astype(BF16)
        state = dot(weighted[:, lanes(h)], grad[:, lanes(h)], 0, 0)
        behind.send[pl.ds(h * HEAD, HEAD)] = state.astype(BF16)

    def norm_out(h):
        total = jnp.zeros((1, HEAD), F32)
        for b in range(BLOCKS):
            at = (rows_of(b), lanes(h))
            scaled_attn = attn[at] * inverse[b]
            normed[at] = (scaled_attn * gain_x[h]).astype(BF16)
            total = total + jnp.sum(cot[at].astype(F32) * scaled_attn, axis=0, keepdims=True)
        term[h] = total

    def spread_term():
        each_peer(X, x, lambda peer: send_row(term.at[peer], term_x.at[x], 6, peer * Z + z))
        term_x[x] = term[x]

    def gather_term():
        wait_for(term_x.at[pl.ds(0, X - 1)], small_sems.at[7])
        whole = term_x[0]
        for n in range(1, X):
            whole = whole + term_x[n]
        term_z[z] = whole
        each_peer(Z, z, lambda peer: send_row(term_z.at[z], term_z.at[z], 8, x * Z + peer))

    def finish_term():
        wait_for(term_z.at[pl.ds(0, Z - 1)], small_sems.at[9])
        whole = term_z[0]
        for n in range(1, Z):
            whole = whole + term_z[n]
        source = lax.broadcasted_iota(jnp.int32, (HEAD, HEAD), 0)
        target = lax.broadcasted_iota(jnp.int32, (HEAD, HEAD), 1)
        pick = (source == target + z * share).astype(F32)
        mine = dot(jnp.broadcast_to(whole, (8, HEAD)), pick, 1, 0, HIGH)
        gg_ref[...] = mine[0:1, 0:share]

    def gradient_part(h):
        masked(h, grad, v, dscore)
        near = below(dscore, h, k)
        far = dot(grad[:, lanes(h)], incoming[pl.ds(h * HEAD, HEAD)], 1, 1)
        for b in range(BLOCKS):
            half, inner = divmod(b * SUB, HALF)
            gq[rows_of(b), lanes(h)] = (
                near[half][inner : inner + SUB] + down(h, b, 1) * far[rows_of(b)]
            ).astype(BF16)
        first, second = above(dscore, h, q)
        gk_part[0:HALF, lanes(h)] = first
        gk_part[HALF:TOK, lanes(h)] = second
        first, second = above(probs, h, grad)
        gv_part[0:HALF, lanes(h)] = first
        gv_part[HALF:TOK, lanes(h)] = second

    def add_later(h):
        state = later[pl.ds(h * HEAD, HEAD)]
        for_k = dot(v[:, lanes(h)], state, 1, 1)
        for_v = dot(k[:, lanes(h)], state, 1, 0)
        for b in range(BLOCKS):
            at = (rows_of(b), lanes(h))
            weight = up(h, b, 1)
            gk[at] = (gk_part[at] + weight * for_k[rows_of(b)]).astype(BF16)
            gv[at] = (gv_part[at] + weight * for_v[rows_of(b)]).astype(BF16)

    back_state(0)
    back_state(1)
    behind.exchange(0)
    back_state(2)
    back_state(3)
    behind.exchange(1)
    for h in range(LOCAL):
        norm_out(h)
    spread_term()
    gradient_part(0)
    behind.total(0)
    gather_term()
    gradient_part(1)
    behind.finish(0)
    behind.total(1)
    gradient_part(2)
    behind.finish(1)
    gradient_part(3)
    finish_term()
    behind.arrived(0)
    add_later(0)
    add_later(1)
    behind.arrived(1)
    add_later(2)
    add_later(3)

    ahead.close()
    behind.close()
    wait_for(gain_z.at[pl.ds(0, Z - 1)], small_sems.at[0])
    wait_for(gain_x.at[pl.ds(0, X - 1)], small_sems.at[2])
    wait_for(norm_parts.at[pl.ds(0, DP - 1)], small_sems.at[4])
    wait_for(term_x.at[pl.ds(0, X - 1)], small_sems.at[6])
    wait_for(term_z.at[pl.ds(0, Z - 1)], small_sems.at[8])


def per_device(Z, DP, queries, keys, values, cotangent, log_decay, gain):
    rows = PAIR // Z
    share = gain.shape[0]
    tokens = pltpu.VMEM((TOK, WIDE), BF16)
    wide = pltpu.VMEM((TOK, WIDE), F32)
    square = pltpu.VMEM((LOCAL, TOK, TOK), BF16)
    scan = [
        pltpu.VMEM((WIDE, HEAD), BF16),
        pltpu.VMEM((2, Z, rows, HEAD), BF16),
        pltpu.VMEM((2, Z, rows, HEAD), F32),
        pltpu.VMEM((2, X, rows, HEAD), F32),
        pltpu.VMEM((2, Z, rows, HEAD), BF16),
        pltpu.VMEM((WIDE, HEAD), BF16),
        pltpu.SemaphoreType.DMA((6, 2)),
    ]
    out = jax.ShapeDtypeStruct((TOK, WIDE), BF16)
    smem, hbm = pl.BlockSpec(memory_space=pltpu.SMEM), pl.BlockSpec(memory_space=pltpu.HBM)
    vmem = pl.BlockSpec(memory_space=pltpu.VMEM)
    normed, gq, gk, gv, gg = pl.pallas_call(
        functools.partial(kernel, Z, DP),
        out_shape=[out, out, out, out, jax.ShapeDtypeStruct((1, share), F32)],
        in_specs=[smem, smem, hbm, hbm, hbm, hbm],
        out_specs=[vmem] * 5,
        scratch_shapes=[tokens] * 6
        + [square, square]
        + [
            pltpu.VMEM((LOCAL, 2, HALF, HALF), F32),
            pltpu.VMEM((LOCAL, SUB, HEAD), F32),
            pltpu.VMEM((LOCAL, SUB, HEAD), F32),
        ]
        + [wide] * 3
        + [
            pltpu.VMEM((DP, 8, HEAD), F32),
            pltpu.VMEM((Z, 1, HEAD), F32),
            pltpu.VMEM((X, 1, HEAD), F32),
            pltpu.VMEM((LOCAL, 1, HEAD), F32),
            pltpu.VMEM((X, 1, HEAD), F32),
            pltpu.VMEM((Z, 1, HEAD), F32),
        ]
        + scan
        + scan
        + [
            pltpu.SemaphoreType.DMA((4,)),
            pltpu.SemaphoreType.DMA((10,)),
        ],
        compiler_params=pltpu.CompilerParams(
            collective_id=0, has_side_effects=True, vmem_limit_bytes=40 * 1024 * 1024
        ),
        cost_estimate=pl.CostEstimate(
            flops=2_000_000_000, bytes_accessed=4_200_000, transcendentals=700_000
        ),
    )(log_decay, gain, queries, keys, values, cotangent)
    return normed, gq, gk, gv, gg.reshape(share)


def solution(mesh):
    both = P("ctx", "dp")
    return jax.shard_map(
        functools.partial(per_device, mesh.shape["ctx"] // X, mesh.shape["dp"]),
        mesh=mesh,
        in_specs=(both, both, both, both, P("dp"), P(("dp", "ctx"))),
        out_specs=(both, both, both, both, P(("dp", "ctx"))),
        check_vma=False,
    )
```

time: 582 us -> 76.7 us (0.13)
  the two profiles are of different devices: /device:TPU:32 before, /device:TPU:2 now
where the time goes in v1:
time: 76.7 us; the launch traced here: 76.4 us
  Pallas kernels  66.5 us (87%)
  local copies, waits for them, and re-layouts  9.15 us (12%)
    pallas_call x1, Pallas kernels, per_device(): pl.pallas_call(functools.partial(kernel, Z, DP), out_shape=[out, out, out...  66.5 us
    unnamed x17, local copies, waits for them, and re-layouts  9.15 us

profile of v1, /device:TPU:2, one launch (start us, length us, event | category | flops | bytes accessed | tf_op | source)
XLA Modules:
  0.0 76.4 jit_solution(3791533955641295128)
XLA Ops:
  0.6 0.0 copy-start
  0.6 1.0 %copy-done = bf16[512,512]{1,0:T(8,128)(2,1)S(1)} copy-done((bf16[512,512]{1,0:T(8,128)(2,1)S(1)}, bf16[512,512]{1,0:T(8,128)(2,1)}, u32[]{:S(2)}) %copy-start) | copy-done | bytes 524312
  1.7 0.0 copy-start.1
  1.7 1.0 %copy-done.1 = bf16[512,512]{1,0:T(8,128)(2,1)S(1)} copy-done((bf16[512,512]{1,0:T(8,128)(2,1)S(1)}, bf16[512,512]{1,0:T(8,128)(2,1)}, u32[]{:S(2)}) %copy-start.1) | copy-done | bytes 524312
  2.7 0.0 copy-start.2
  2.7 1.0 %copy-done.2 = bf16[512,512]{1,0:T(8,128)(2,1)S(1)} copy-done((bf16[512,512]{1,0:T(8,128)(2,1)S(1)}, bf16[512,512]{1,0:T(8,128)(2,1)}, u32[]{:S(2)}) %copy-start.2) | copy-done | bytes 524312
  3.8 0.0 copy-start.3
  3.8 1.0 %copy-done.3 = bf16[512,512]{1,0:T(8,128)(2,1)S(1)} copy-done((bf16[512,512]{1,0:T(8,128)(2,1)S(1)}, bf16[512,512]{1,0:T(8,128)(2,1)}, u32[]{:S(2)}) %copy-start.3) | copy-done | bytes 524312
  4.8 0.0 copy-start.4
  4.8 0.7 copy-done.4
  5.5 0.0 copy-start.5
  5.5 0.7 copy-done.5
  6.1 66.5 %shard_map.101 = (bf16[512,512]{1,0:T(8,128)(2,1)S(1)}, bf16[512,512]{1,0:T(8,128)(2,1)S(1)}, bf16[512,512]{1,0:T(8,128)(2,1)S(1)}, bf16[512,512]{1,0:T(8,128)(2,1)S(1)}, f32[1,8]{1,0:T(1,128)S(1)}) custom-call(f32[4]{0:T(128)S(1)} %copy-done.4, f32[8]{0:T(128)S(1)} %copy-done.5, bf16[512,512]{1,0:T(8,128)(2,1)S(1)} %copy-done, ...), custom_call_target="tpu_custom_call" | custom-call | flops 2000000000 | bytes 4200000 | tf_op jit(solution)/shard_map/pallas_call | solution.py:517
  72.7 0.8 %copy.16 = bf16[512,512]{1,0:T(8,128)(2,1)} copy(bf16[512,512]{1,0:T(8,128)(2,1)S(1)} %get-tuple-element.20) | data formatting | bytes 1048576
  73.5 0.8 %copy.17 = bf16[512,512]{1,0:T(8,128)(2,1)} copy(bf16[512,512]{1,0:T(8,128)(2,1)S(1)} %get-tuple-element.21) | data formatting | bytes 1048576
  74.3 0.8 %copy.18 = bf16[512,512]{1,0:T(8,128)(2,1)} copy(bf16[512,512]{1,0:T(8,128)(2,1)S(1)} %get-tuple-element.22) | data formatting | bytes 1048576
  75.1 0.8 %copy.19 = bf16[512,512]{1,0:T(8,128)(2,1)} copy(bf16[512,512]{1,0:T(8,128)(2,1)S(1)} %get-tuple-element.23) | data formatting | bytes 1048576
  75.8 0.5 copy.20
Async XLA Ops:
  0.6 1.0 %copy-start = (bf16[512,512]{1,0:T(8,128)(2,1)S(1)}, bf16[512,512]{1,0:T(8,128)(2,1)}, u32[]{:S(2)}) copy-start(bf16[512,512]{1,0:T(8,128)(2,1)} %q_hbm.1) | copy-start | bytes 1572868
  1.7 1.0 %copy-start.1 = (bf16[512,512]{1,0:T(8,128)(2,1)S(1)}, bf16[512,512]{1,0:T(8,128)(2,1)}, u32[]{:S(2)}) copy-start(bf16[512,512]{1,0:T(8,128)(2,1)} %k_hbm.1) | copy-start | bytes 1572868
  2.7 1.0 %copy-start.2 = (bf16[512,512]{1,0:T(8,128)(2,1)S(1)}, bf16[512,512]{1,0:T(8,128)(2,1)}, u32[]{:S(2)}) copy-start(bf16[512,512]{1,0:T(8,128)(2,1)} %v_hbm.1) | copy-start | bytes 1572868
  3.8 1.0 %copy-start.3 = (bf16[512,512]{1,0:T(8,128)(2,1)S(1)}, bf16[512,512]{1,0:T(8,128)(2,1)}, u32[]{:S(2)}) copy-start(bf16[512,512]{1,0:T(8,128)(2,1)} %cot_hbm.1) | copy-start | bytes 1572868
  4.8 0.7 copy-start.4
  5.5 0.7 copy-start.5

commit v2 on v1

--- a/solution.py
+++ b/solution.py
@@ -30,12 +30,9 @@
 
 
 def each_peer(count, me, body):
-    def step(i, carry):
-        offset = count // 2 + ((i + 1) // 2) * (1 - 2 * lax.rem(i, 2))
+    for i in range(count - 1):
+        offset = count // 2 + ((i + 1) // 2) * (1 - 2 * (i % 2))
         body(lax.rem(me + offset, count))
-        return carry
-
-    lax.fori_loop(0, count - 1, step, 0)
 
 
 def wait_for(ref, sem):
@@ -48,110 +45,100 @@
         self.rate_ref = rate_ref
         self.backward = backward
         self.send, self.gather, self.pre, self.totals, self.back, self.result, self.sems = refs
-        self.rows = PAIR // self.Z
-
-    def sem(self, kind, j):
-        return self.sems.at[kind, j]
-
-    def rate(self, j):
-        return self.rate_ref[2 * j + self.z // (self.Z // 2)]
-
-    def exchange(self, j):
-        rows, z = self.rows, self.z
-
-        def one(peer):
-            pltpu.make_async_remote_copy(
-                src_ref=self.send.at[pl.ds(pl.multiple_of(j * PAIR + peer * rows, rows), rows)],
-                dst_ref=self.gather.at[j, z],
-                send_sem=self.sem(0, j),
-                recv_sem=self.sem(1, j),
-                device_id={"ctx": self.x * self.Z + peer},
-                device_id_type=MESH,
-            ).start()
-
-        each_peer(self.Z, z, one)
-        own = self.send[pl.ds(pl.multiple_of(j * PAIR + z * rows, rows), rows)]
-        self.gather[j, z] = own
-
-    def total(self, j):
+        self.rows = WIDE // self.Z
+
+    def piece(self, ref, place):
+        return ref.at[pl.ds(pl.multiple_of(place * self.rows, self.rows), self.rows)]
+
+    def rate(self):
+        return self.rate_ref[self.z // (self.Z // LOCAL)]
+
+    def order(self):
+        return range(self.Z - 1, -1, -1) if self.backward else range(self.Z)
+
+    def copy(self, source, target, step, ctx):
+        pltpu.make_async_remote_copy(
+            src_ref=source,
+            dst_ref=target,
+            send_sem=self.sems.at[2 * step],
+            recv_sem=self.sems.at[2 * step + 1],
+            device_id={"ctx": ctx},
+            device_id_type=MESH,
+        ).start()
+
+    def exchange(self):
+        mine = self.gather.at[self.z]
+        each_peer(
+            self.Z,
+            self.z,
+            lambda peer: self.copy(self.piece(self.send, peer), mine, 0, self.x * self.Z + peer),
+        )
+        mine[...] = self.piece(self.send, self.z)[...]
+
+    def total(self):
         rows, x = self.rows, self.x
-        wait_for(self.gather.at[j, pl.ds(0, self.Z - 1)], self.sem(1, j))
-        decay = jnp.exp(jnp.full((rows, HEAD), -float(TOK) * self.rate(j), F32))
+        wait_for(self.gather.at[pl.ds(0, self.Z - 1)], self.sems.at[1])
+        decay = jnp.exp(jnp.full((rows, HEAD), -float(TOK) * self.rate(), F32))
         state = jnp.zeros((rows, HEAD), F32)
-        order = range(self.Z - 1, -1, -1) if self.backward else range(self.Z)
-        for place in order:
-            self.pre[j, place] = state
-            state = decay * state + self.gather[j, place].astype(F32)
-        self.totals[j, x] = state
-
-        def one(peer):
-            pltpu.make_async_remote_copy(
-                src_ref=self.totals.at[j, x],
-                dst_ref=self.totals.at[j, x],
-                send_sem=self.sem(2, j),
-                recv_sem=self.sem(3, j),
-                device_id={"ctx": peer * self.Z + self.z},
-                device_id_type=MESH,
-            ).start()
-
-        each_peer(X, x, one)
-
-    def finish(self, j):
-        rows, x, z = self.rows, self.x, self.z
-        wait_for(self.totals.at[j, pl.ds(0, X - 1)], self.sem(3, j))
-        rate = self.rate(j)
+        for place in self.order():
+            self.pre[place] = state
+            state = decay * state + self.gather[place].astype(F32)
+        self.totals[x] = state
+        mine = self.totals.at[x]
+        each_peer(X, x, lambda peer: self.copy(mine, mine, 1, peer * self.Z + self.z))
+
+    def finish(self):
+        rows, x = self.rows, self.x
+        wait_for(self.totals.at[pl.ds(0, X - 1)], self.sems.at[3])
+        rate = self.rate()
         far = jnp.zeros((rows, HEAD), F32)
         for other in range(X):
             steps = (other - x - 1) if self.backward else (x - other - 1)
             reach = jnp.maximum(steps, 0).astype(F32) * (float(TOK) * self.Z)
             weight = jnp.exp(jnp.full((rows, HEAD), -reach * rate, F32))
-            far = far + jnp.where(steps >= 0, weight * self.totals[j, other], 0.0)
+            far = far + jnp.where(steps >= 0, weight * self.totals[other], 0.0)
         decay = jnp.exp(jnp.full((rows, HEAD), -float(TOK) * rate, F32))
-        order = range(self.Z - 1, -1, -1) if self.backward else range(self.Z)
-        for place in order:
-            self.back[j, place] = (self.pre[j, place] + far).astype(BF16)
+        for place in self.order():
+            self.back[place] = (self.pre[place] + far).astype(BF16)
             far = far * decay
-
-        def one(peer):
-            pltpu.make_async_remote_copy(
-                src_ref=self.back.at[j, peer],
-                dst_ref=self.result.at[pl.ds(pl.multiple_of(j * PAIR + z * rows, rows), rows)],
-                send_sem=self.sem(4, j),
-                recv_sem=self.sem(5, j),
-                device_id={"ctx": x * self.Z + peer},
-                device_id_type=MESH,
-            ).start()
-
-        each_peer(self.Z, z, one)
-        self.result[pl.ds(pl.multiple_of(j * PAIR + z * rows, rows), rows)] = self.back[j, z]
-
-    def arrived(self, j):
-        wait_for(self.back.at[j, pl.ds(0, self.Z - 1)], self.sem(5, j))
+        mine = self.piece(self.result, self.z)
+        each_peer(
+            self.Z,
+            self.z,
+            lambda peer: self.copy(self.back.at[peer], mine, 2, x * self.Z + peer),
+        )
+        mine[...] = self.back[self.z]
+
+    def arrived(self):
+        wait_for(self.back.at[pl.ds(0, self.Z - 1)], self.sems.at[5])
 
     def close(self):
-        for j in range(2):
-            wait_for(self.gather.at[j, pl.ds(0, self.Z - 1)], self.sem(0, j))
-            wait_for(self.totals.at[j, pl.ds(0, X - 1)], self.sem(2, j))
-            wait_for(self.back.at[j, pl.ds(0, self.Z - 1)], self.sem(4, j))
+        wait_for(self.gather.at[pl.ds(0, self.Z - 1)], self.sems.at[0])
+        wait_for(self.totals.at[pl.ds(0, X - 1)], self.sems.at[2])
+        wait_for(self.back.at[pl.ds(0, self.Z - 1)], self.sems.at[4])
 
 
 def kernel(
     Z,
     DP,
-    rate_ref,
-    gain_ref,
+    rate_hbm,
+    gain_hbm,
     q_hbm,
     k_hbm,
     v_hbm,
     cot_hbm,
+    k,
+    v,
     normed,
     gq,
-    gk,
-    gv,
+    gk_part,
+    gv_part,
+    rest_weight,
+    later_out,
     gg_ref,
+    rate_ref,
+    gain_ref,
     q,
-    k,
-    v,
     cot,
     grad,
     weighted,
@@ -161,8 +148,6 @@
     down_base,
     up_base,
     attn,
-    gk_part,
-    gv_part,
     norm_parts,
     gain_z,
     gain_x,
@@ -178,15 +163,6 @@
     channels = DP * WIDE
     share = WIDE // (X * Z)
 
-    loads = [
-        pltpu.make_async_copy(source, target, load_sems.at[i])
-        for i, (source, target) in enumerate(
-            ((k_hbm, k), (v_hbm, v), (q_hbm, q), (cot_hbm, cot))
-        )
-    ]
-    for load in loads:
-        load.start()
-
     barrier = pltpu.get_barrier_semaphore()
 
     def greet_row(peer):
@@ -205,6 +181,21 @@
     each_peer(Z, z, greet_row)
     each_peer(X, x, greet_rows)
     each_peer(DP, d, greet_dp)
+
+    sources = ((k_hbm, k), (v_hbm, v), (q_hbm, q), (cot_hbm, cot))
+    small_loads = [
+        pltpu.make_async_copy(rate_hbm, rate_ref, load_sems.at[4]),
+        pltpu.make_async_copy(gain_hbm, gain_ref, load_sems.at[5]),
+    ]
+    for load in small_loads:
+        load.start()
+    for i, (source, target) in enumerate(sources):
+        for b in range(BLOCKS):
+            part = pl.ds(b * SUB, SUB)
+            pltpu.make_async_copy(source.at[part], target.at[part], load_sems.at[i]).start()
+
+    def loaded(i):
+        wait_for(sources[i][1], load_sems.at[i])
 
     place = (x, z, Z)
     ahead = Scan(place, rate_ref, False, forward_refs)
@@ -243,7 +234,6 @@
         mask[h, 1] = jnp.exp(-rate_ref[h] * (offset + float(HALF)))
 
     def block_state(h):
-        make_up(h)
         weighted_k = jnp.concatenate(
             [
                 (k[rows_of(b), lanes(h)].astype(F32) * up(h, b)).astype(BF16)
@@ -287,6 +277,7 @@
             weighted[rows_of(b), lanes(h)] = (
                 q[rows_of(b), lanes(h)].astype(F32) * down(h, b)
             ).astype(BF16)
+            rest_weight[h, rows_of(b)] = up(h, b, 1)
 
     def add_remote(h):
         remote = dot(q[:, lanes(h)], incoming[pl.ds(h * HEAD, HEAD)], 1, 0)
@@ -323,38 +314,30 @@
     def gain_arrived():
         wait_for(gain_x.at[pl.ds(0, X - 1)], small_sems.at[3])
 
-    loads[0].wait()
-    loads[1].wait()
-    block_state(0)
-    block_state(1)
+    small_loads[0].wait()
+    for h in range(LOCAL):
+        make_up(h)
+    loaded(0)
+    loaded(1)
+    for h in range(LOCAL):
+        block_state(h)
+    small_loads[1].wait()
     pl.semaphore_wait(barrier, (Z - 1) + (X - 1) + (DP - 1))
-    ahead.exchange(0)
-    block_state(2)
-    block_state(3)
-    ahead.exchange(1)
+    ahead.exchange()
     gather_gain()
-    loads[2].wait()
-    local_part(0)
-    local_part(1)
-    ahead.total(0)
-    weigh_queries(0)
-    weigh_queries(1)
-    ahead.finish(0)
-    ahead.total(1)
+    loaded(2)
+    for h in range(LOCAL):
+        local_part(h)
+    for h in range(LOCAL):
+        weigh_queries(h)
+    loaded(3)
+    ahead.total()
     spread_gain()
-    local_part(2)
-    ahead.finish(1)
-    local_part(3)
-    weigh_queries(2)
-    weigh_queries(3)
-    loads[3].wait()
+    ahead.finish()
     gain_arrived()
-    ahead.arrived(0)
-    add_remote(0)
-    add_remote(1)
-    ahead.arrived(1)
-    add_remote(2)
-    add_remote(3)
+    ahead.arrived()
+    for h in range(LOCAL):
+        add_remote(h)
 
     ones = jnp.ones((8, HEAD), F32)
     row8 = lax.broadcasted_iota(jnp.int32, (8, HEAD), 0)
@@ -451,41 +434,22 @@
         gv_part[0:HALF, lanes(h)] = first
         gv_part[HALF:TOK, lanes(h)] = second
 
-    def add_later(h):
-        state = later[pl.ds(h * HEAD, HEAD)]
-        for_k = dot(v[:, lanes(h)], state, 1, 1)
-        for_v = dot(k[:, lanes(h)], state, 1, 0)
-        for b in range(BLOCKS):
-            at = (rows_of(b), lanes(h))
-            weight = up(h, b, 1)
-            gk[at] = (gk_part[at] + weight * for_k[rows_of(b)]).astype(BF16)
-            gv[at] = (gv_part[at] + weight * for_v[rows_of(b)]).astype(BF16)
-
-    back_state(0)
-    back_state(1)
-    behind.exchange(0)
-    back_state(2)
-    back_state(3)
-    behind.exchange(1)
+    for h in range(LOCAL):
+        back_state(h)
+    behind.exchange()
     for h in range(LOCAL):
         norm_out(h)
     spread_term()
     gradient_part(0)
-    behind.total(0)
+    gradient_part(1)
     gather_term()
-    gradient_part(1)
-    behind.finish(0)
-    behind.total(1)
     gradient_part(2)
-    behind.finish(1)
     gradient_part(3)
+    behind.total()
+    behind.finish()
     finish_term()
-    behind.arrived(0)
-    add_later(0)
-    add_later(1)
-    behind.arrived(1)
-    add_later(2)
-    add_later(3)
+    behind.arrived()
+    later_out[...] = later[...]
 
     ahead.close()
     behind.close()
@@ -496,38 +460,97 @@
     wait_for(term_z.at[pl.ds(0, Z - 1)], small_sems.at[8])
 
 
+def writer(
+    k,
+    v,
+    normed,
+    gq,
+    gk_part,
+    gv_part,
+    rest_weight,
+    later,
+    gain_sum,
+    normed_hbm,
+    gq_hbm,
+    gk_hbm,
+    gv_hbm,
+    gg_hbm,
+    gk,
+    gv,
+    sems,
+):
+    pltpu.make_async_copy(gain_sum, gg_hbm, sems.at[4]).start()
+
+    def write(i, source, target, b):
+        part = pl.ds(b * SUB, SUB)
+        pltpu.make_async_copy(source.at[part], target.at[part], sems.at[i]).start()
+
+    for b in range(BLOCKS):
+        write(0, normed, normed_hbm, b)
+        write(1, gq, gq_hbm, b)
+    for b in range(BLOCKS):
+        rows = slice(b * SUB, (b + 1) * SUB)
+        for h in range(LOCAL):
+            at = (rows, slice(h * HEAD, (h + 1) * HEAD))
+            state = later[pl.ds(h * HEAD, HEAD)]
+            weight = rest_weight[h, rows]
+            gk[at] = (gk_part[at] + weight * dot(v[at], state, 1, 1)).astype(BF16)
+            gv[at] = (gv_part[at] + weight * dot(k[at], state, 1, 0)).astype(BF16)
+        write(2, gk, gk_hbm, b)
+        write(3, gv, gv_hbm, b)
+    for i, whole in enumerate((normed, gq, gk, gv, gain_sum)):
+        wait_for(whole, sems.at[i])
+
+
 def per_device(Z, DP, queries, keys, values, cotangent, log_decay, gain):
-    rows = PAIR // Z
+    rows = WIDE // Z
     share = gain.shape[0]
     tokens = pltpu.VMEM((TOK, WIDE), BF16)
-    wide = pltpu.VMEM((TOK, WIDE), F32)
     square = pltpu.VMEM((LOCAL, TOK, TOK), BF16)
     scan = [
         pltpu.VMEM((WIDE, HEAD), BF16),
-        pltpu.VMEM((2, Z, rows, HEAD), BF16),
-        pltpu.VMEM((2, Z, rows, HEAD), F32),
-        pltpu.VMEM((2, X, rows, HEAD), F32),
-        pltpu.VMEM((2, Z, rows, HEAD), BF16),
+        pltpu.VMEM((Z, rows, HEAD), BF16),
+        pltpu.VMEM((Z, rows, HEAD), F32),
+        pltpu.VMEM((X, rows, HEAD), F32),
+        pltpu.VMEM((Z, rows, HEAD), BF16),
         pltpu.VMEM((WIDE, HEAD), BF16),
-        pltpu.SemaphoreType.DMA((6, 2)),
+        pltpu.SemaphoreType.DMA((6,)),
     ]
-    out = jax.ShapeDtypeStruct((TOK, WIDE), BF16)
-    smem, hbm = pl.BlockSpec(memory_space=pltpu.SMEM), pl.BlockSpec(memory_space=pltpu.HBM)
+    half, full = jax.ShapeDtypeStruct((TOK, WIDE), BF16), jax.ShapeDtypeStruct((TOK, WIDE), F32)
+    hbm = pl.BlockSpec(memory_space=pltpu.HBM)
     vmem = pl.BlockSpec(memory_space=pltpu.VMEM)
-    normed, gq, gk, gv, gg = pl.pallas_call(
+    inputs = [
+        pltpu.with_memory_space_constraint(array, pltpu.HBM)
+        for array in (log_decay, gain, queries, keys, values, cotangent)
+    ]
+    held = pl.pallas_call(
         functools.partial(kernel, Z, DP),
-        out_shape=[out, out, out, out, jax.ShapeDtypeStruct((1, share), F32)],
-        in_specs=[smem, smem, hbm, hbm, hbm, hbm],
-        out_specs=[vmem] * 5,
-        scratch_shapes=[tokens] * 6
-        + [square, square]
-        + [
+        out_shape=[
+            half,
+            half,
+            half,
+            half,
+            full,
+            full,
+            jax.ShapeDtypeStruct((LOCAL, TOK, HEAD), F32),
+            jax.ShapeDtypeStruct((WIDE, HEAD), BF16),
+            jax.ShapeDtypeStruct((1, share), F32),
+        ],
+        in_specs=[hbm] * 6,
+        out_specs=[vmem] * 9,
+        scratch_shapes=[
+            pltpu.SMEM((LOCAL,), F32),
+            pltpu.SMEM((share,), F32),
+            tokens,
+            tokens,
+            tokens,
+            tokens,
+            square,
+            square,
             pltpu.VMEM((LOCAL, 2, HALF, HALF), F32),
             pltpu.VMEM((LOCAL, SUB, HEAD), F32),
             pltpu.VMEM((LOCAL, SUB, HEAD), F32),
-        ]
-        + [wide] * 3
-        + [
+            pltpu.VMEM((TOK, WIDE), F32),
             pltpu.VMEM((DP, 8, HEAD), F32),
             pltpu.VMEM((Z, 1, HEAD), F32),
             pltpu.VMEM((X, 1, HEAD), F32),
@@ -537,17 +560,25 @@
         ]
         + scan
         + scan
-        + [
-            pltpu.SemaphoreType.DMA((4,)),
-            pltpu.SemaphoreType.DMA((10,)),
-        ],
+        + [pltpu.SemaphoreType.DMA((6,)), pltpu.SemaphoreType.DMA((10,))],
         compiler_params=pltpu.CompilerParams(
             collective_id=0, has_side_effects=True, vmem_limit_bytes=40 * 1024 * 1024
         ),
         cost_estimate=pl.CostEstimate(
             flops=2_000_000_000, bytes_accessed=4_200_000, transcendentals=700_000
         ),
-    )(log_decay, gain, queries, keys, values, cotangent)
+    )(*inputs)
+    normed, gq, gk, gv, gg = pl.pallas_call(
+        writer,
+        out_shape=[half, half, half, half, jax.ShapeDtypeStruct((1, share), F32)],
+        in_specs=[vmem] * 9,
+        out_specs=[hbm] * 5,
+        scratch_shapes=[tokens, tokens, pltpu.SemaphoreType.DMA((5,))],
+        compiler_params=pltpu.CompilerParams(vmem_limit_bytes=24 * 1024 * 1024),
+        cost_estimate=pl.CostEstimate(
+            flops=300_000_000, bytes_accessed=2_200_000, transcendentals=0
+        ),
+    )(*held)
     return normed, gq, gk, gv, gg.reshape(share)
 
 

time: 76.7 us -> 63.9 us (0.83)
  local copies, waits for them, and re-layouts: 9.15 us -> 0 us
  Pallas kernels: 66.5 us -> 63.1 us
    unnamed x17 -> x0, local copies, waits for them, and re-layouts: 9.15 us -> none
    pallas_call x1 -> x2, Pallas kernels: 66.5 us -> 63.1 us  [the longest x1 61.8 us: per_device(): pl.pallas_call(functools.partial(kernel, Z, DP), out_shape=[half, half, h...]
where the time goes in v2:
time: 63.9 us; the launch traced here: 63.8 us
  Pallas kernels  63.1 us (99%)
  between operations  0.64 us (1%)
    pallas_call x1, Pallas kernels, per_device(): pl.pallas_call(functools.partial(kernel, Z, DP), out_shape=[half, half, h...  61.8 us
    pallas_call x1, Pallas kernels, per_device(): pl.pallas_call(writer, out_shape=[half, half, half, half, jax.ShapeDtypeS...  1.35 us

profile of v2, /device:TPU:2, one launch (start us, length us, event | category | flops | bytes accessed | tf_op | source)
XLA Modules:
  0.0 63.8 jit_solution(10621212225180956743)
XLA Ops:
  0.6 61.8 %shard_map.101 = (bf16[512,512]{1,0:T(8,128)(2,1)S(1)}, bf16[512,512]{1,0:T(8,128)(2,1)S(1)}, bf16[512,512]{1,0:T(8,128)(2,1)S(1)}, bf16[512,512]{1,0:T(8,128)(2...) custom-call(f32[4]{0:T(128)} %rate_hbm.1, ...), custom_call_target="tpu_custom_call" | custom-call | flops 2000000000 | bytes 4200000 | tf_op jit(solution)/shard_map/pallas_call | solution.py:526
  62.4 1.3 %shard_map.102 = (bf16[512,512]{1,0:T(8,128)(2,1)}, bf16[512,512]{1,0:T(8,128)(2,1)}, bf16[512,512]{1,0:T(8,128)(2,1)}, bf16[512,512]{1,0:T(8,128)(2,1)}, f32[1,8]{1,0:T(1,128)}) custom-call(bf16[512,512]{1,0:T(8,128)(2,1)S(1)} %get-tuple-element.19.k, bf16[512,512]{1,0:T(8,128)(2,1)S(1)} %get-tuple-element.20.v, ...), custom_call_target="tpu_custom_call" | custom-call | flops 300000000 | bytes 2200000 | tf_op jit(solution)/shard_map/pallas_call | solution.py:571

commit v3 on v2

--- a/solution.py
+++ b/solution.py
@@ -15,7 +15,9 @@
 BLOCKS = TOK // SUB
 HALF = 256
 X = 4
-PAIR = 2 * HEAD
+WINDOW = 4
+PIECE = HEAD // WINDOW
+NEAR = (0, 1, -1, -2)
 
 eps_norm = 1e-06
 F32, BF16 = jnp.float32, jnp.bfloat16
@@ -33,6 +35,11 @@
     for i in range(count - 1):
         offset = count // 2 + ((i + 1) // 2) * (1 - 2 * (i % 2))
         body(lax.rem(me + offset, count))
+
+
+def near_places(steps):
+    pairs = [(a, b) for a in range(X) for b in steps if (a, b) != (0, 0)]
+    return sorted(pairs, key=lambda p: -(min(p[0], X - p[0]) + abs(p[1])))
 
 
 def wait_for(ref, sem):
@@ -44,78 +51,117 @@
         self.x, self.z, self.Z = place
         self.rate_ref = rate_ref
         self.backward = backward
-        self.send, self.gather, self.pre, self.totals, self.back, self.result, self.sems = refs
-        self.rows = WIDE // self.Z
-
-    def piece(self, ref, place):
-        return ref.at[pl.ds(pl.multiple_of(place * self.rows, self.rows), self.rows)]
-
-    def rate(self):
-        return self.rate_ref[self.z // (self.Z // LOCAL)]
-
-    def order(self):
-        return range(self.Z - 1, -1, -1) if self.backward else range(self.Z)
-
-    def copy(self, source, target, step, ctx):
+        self.send, self.gather, self.inner, self.own, self.out, self.far, self.outer = refs[:7]
+        self.back, self.result, self.sems = refs[7:]
+        self.first = lax.rem(self.z + self.Z - 2, self.Z)
+        self.shift = [(self.first + q) // self.Z for q in range(WINDOW)]
+        self.ring = range(WINDOW, self.Z, WINDOW)
+
+    def clear(self):
+        zero = jnp.zeros((PIECE, HEAD), F32)
+        for q in range(WINDOW):
+            self.gather[q, 0] = zero.astype(BF16)
+            self.gather[q, X + 1] = zero.astype(BF16)
+        for j in range(len(self.ring)):
+            for i in (0, 1, X + 1, X + 2):
+                self.far[j, i] = zero.astype(BF16)
+        self.own[0] = zero
+        self.own[X + 2] = zero
+
+    def piece(self, ref, x, z):
+        start = (x * WINDOW + lax.rem(z, WINDOW)) * PIECE
+        return ref.at[pl.ds(pl.multiple_of(start, PIECE), PIECE)]
+
+    def decay(self, blocks):
+        return jnp.exp(jnp.full((1, HEAD), -float(TOK * blocks) * self.rate_ref[self.x], F32))
+
+    def copy(self, source, target, step, x, z):
         pltpu.make_async_remote_copy(
             src_ref=source,
             dst_ref=target,
             send_sem=self.sems.at[2 * step],
             recv_sem=self.sems.at[2 * step + 1],
-            device_id={"ctx": ctx},
+            device_id={"ctx": x * self.Z + z},
             device_id_type=MESH,
         ).start()
 
+    def at(self, a, b):
+        return lax.rem(self.x + a, X), lax.rem(self.z + b + self.Z, self.Z)
+
+    def wait_near(self, sem):
+        wait_for(self.gather.at[pl.ds(0, 3), pl.ds(0, 5)], self.sems.at[sem])
+
+    def wait_far(self, sem):
+        wait_for(self.far.at[:, pl.ds(0, X)], self.sems.at[sem])
+
     def exchange(self):
-        mine = self.gather.at[self.z]
-        each_peer(
-            self.Z,
-            self.z,
-            lambda peer: self.copy(self.piece(self.send, peer), mine, 0, self.x * self.Z + peer),
-        )
-        mine[...] = self.piece(self.send, self.z)[...]
+        for a in (2, 1, 3, 0):
+            self.exchange_with(a)
+        self.keep()
+
+    def exchange_with(self, a):
+        for b in (2, 1, -1, 0):
+            if (a, b) != (0, 0):
+                x, z = self.at(a, b)
+                self.copy(self.piece(self.send, x, z), self.gather.at[2 - b, self.x + 1], 0, x, z)
+
+    def keep(self):
+        self.gather[2, self.x + 1] = self.piece(self.send, self.x, self.z)[...]
 
     def total(self):
-        rows, x = self.rows, self.x
-        wait_for(self.gather.at[pl.ds(0, self.Z - 1)], self.sems.at[1])
-        decay = jnp.exp(jnp.full((rows, HEAD), -float(TOK) * self.rate(), F32))
-        state = jnp.zeros((rows, HEAD), F32)
-        for place in self.order():
-            self.pre[place] = state
-            state = decay * state + self.gather[place].astype(F32)
-        self.totals[x] = state
-        mine = self.totals.at[x]
-        each_peer(X, x, lambda peer: self.copy(mine, mine, 1, peer * self.Z + self.z))
+        decay, row_decay = self.decay(1), self.decay(self.Z)
+        instances, slots = range(X + 1), range(WINDOW)
+        if self.backward:
+            instances, slots = instances[::-1], slots[::-1]
+        self.wait_near(1)
+        running = jnp.zeros((PIECE, HEAD), F32)
+        for i in instances:
+            state = jnp.zeros((PIECE, HEAD), F32)
+            for q in slots:
+                self.inner[i, q] = state
+                state = decay * state + self.gather[q, i + self.shift[q]].astype(F32)
+            running = row_decay * running + state
+            self.own[i + 1] = running
+            self.out[i] = running.astype(BF16)
+        for j, distance in sorted(enumerate(self.ring), key=lambda p: -min(p[1], self.Z - p[1])):
+            x, z = self.at(0, distance)
+            start = 1 if self.backward else jnp.where(self.first + distance < self.Z, 1, 0)
+            self.copy(self.out.at[pl.ds(start, X)], self.far.at[j, pl.ds(start + 1, X)], 1, x, z)
 
     def finish(self):
-        rows, x = self.rows, self.x
-        wait_for(self.totals.at[pl.ds(0, X - 1)], self.sems.at[3])
-        rate = self.rate()
-        far = jnp.zeros((rows, HEAD), F32)
-        for other in range(X):
-            steps = (other - x - 1) if self.backward else (x - other - 1)
-            reach = jnp.maximum(steps, 0).astype(F32) * (float(TOK) * self.Z)
-            weight = jnp.exp(jnp.full((rows, HEAD), -reach * rate, F32))
-            far = far + jnp.where(steps >= 0, weight * self.totals[other], 0.0)
-        decay = jnp.exp(jnp.full((rows, HEAD), -float(TOK) * rate, F32))
-        for place in self.order():
-            self.back[place] = (self.pre[place] + far).astype(BF16)
-            far = far * decay
-        mine = self.piece(self.result, self.z)
-        each_peer(
-            self.Z,
-            self.z,
-            lambda peer: self.copy(self.back.at[peer], mine, 2, x * self.Z + peer),
-        )
-        mine[...] = self.back[self.z]
+        gaps, offsets = [], []
+        for distance in self.ring:
+            if self.backward:
+                gaps.append(self.decay(self.Z - distance - WINDOW))
+                offsets.append(1 + jnp.where(self.first < distance, 0, 1))
+            else:
+                gaps.append(self.decay(distance - WINDOW))
+                offsets.append(1 - jnp.where(self.first >= distance, 0, 1))
+        own_gap = self.decay(self.Z - WINDOW)
+        reach = [self.decay(WINDOW - 1 - q if self.backward else q) for q in range(WINDOW)]
+        self.wait_far(3)
+        for i in range(X + 1):
+            total = own_gap * self.own[i + 2 if self.backward else i]
+            for j, (gap, offset) in enumerate(zip(gaps, offsets)):
+                total = total + gap * self.far[j, i + offset].astype(F32)
+            self.outer[i] = total
+        for x in range(X):
+            for q in range(WINDOW):
+                i = x + 1 - self.shift[q]
+                self.back[x, q] = (reach[q] * self.outer[i] + self.inner[i, q]).astype(BF16)
+        mine = self.piece(self.result, self.x, self.z)
+        for a, b in near_places((-2, -1, 0, 1)):
+            x, z = self.at(a, b)
+            self.copy(self.back.at[x, b + 2], mine, 2, x, z)
+        mine[...] = self.back[self.x, 2]
 
     def arrived(self):
-        wait_for(self.back.at[pl.ds(0, self.Z - 1)], self.sems.at[5])
+        self.wait_near(5)
 
     def close(self):
-        wait_for(self.gather.at[pl.ds(0, self.Z - 1)], self.sems.at[0])
-        wait_for(self.totals.at[pl.ds(0, X - 1)], self.sems.at[2])
-        wait_for(self.back.at[pl.ds(0, self.Z - 1)], self.sems.at[4])
+        self.wait_near(0)
+        self.wait_far(2)
+        self.wait_near(4)
 
 
 def kernel(
@@ -148,38 +194,54 @@
     down_base,
     up_base,
     attn,
+    cot_gain,
     norm_parts,
-    gain_z,
+    gain_near,
+    gain_far,
     gain_x,
     term,
     term_x,
-    term_z,
+    term_near,
+    term_far,
     *rest,
 ):
-    forward_refs, backward_refs = rest[0:7], rest[7:14]
-    load_sems, small_sems = rest[14:]
+    forward_refs, backward_refs = rest[0:10], rest[10:20]
+    load_sems, small_sems, relay = rest[20:]
     ctx, d = lax.axis_index("ctx"), lax.axis_index("dp")
     x, z = ctx // Z, lax.rem(ctx, Z)
     channels = DP * WIDE
     share = WIDE // (X * Z)
 
+    place = (x, z, Z)
+    ahead = Scan(place, rate_ref, False, forward_refs)
+    behind = Scan(place, rate_ref, True, backward_refs)
+    incoming, later = ahead.result, behind.result
+    ahead.clear()
+    behind.clear()
+
     barrier = pltpu.get_barrier_semaphore()
 
-    def greet_row(peer):
-        pl.semaphore_signal(
-            barrier, inc=1, device_id={"ctx": x * Z + peer}, device_id_type=MESH
-        )
-
-    def greet_rows(peer):
-        pl.semaphore_signal(
-            barrier, inc=1, device_id={"ctx": peer * Z + z}, device_id_type=MESH
-        )
+    def ring(b):
+        return lax.rem(z + b + Z, Z)
+
+    far_steps = range(WINDOW, Z, WINDOW)
+    near = near_places((2, 1, 0, -1, -2))
+    for a, b in near:
+        target = lax.rem(x + a, X) * Z + ring(b)
+        pl.semaphore_signal(barrier, inc=1, device_id={"ctx": target}, device_id_type=MESH)
+
+    def tell(n, steps):
+        for b in (steps, -steps):
+            pl.semaphore_signal(
+                relay.at[n], inc=1, device_id={"ctx": x * Z + ring(b)}, device_id_type=MESH
+            )
+
+    def told(n):
+        pl.semaphore_wait(relay.at[n], 2)
 
     def greet_dp(peer):
         pl.semaphore_signal(barrier, inc=1, device_id={"dp": peer}, device_id_type=MESH)
 
-    each_peer(Z, z, greet_row)
-    each_peer(X, x, greet_rows)
     each_peer(DP, d, greet_dp)
 
     sources = ((k_hbm, k), (v_hbm, v), (q_hbm, q), (cot_hbm, cot))
@@ -197,13 +259,8 @@
     def loaded(i):
         wait_for(sources[i][1], load_sems.at[i])
 
-    place = (x, z, Z)
-    ahead = Scan(place, rate_ref, False, forward_refs)
-    behind = Scan(place, rate_ref, True, backward_refs)
-    incoming, later = ahead.result, behind.result
-
     def lanes(h):
-        return slice(h * HEAD, (h + 1) * HEAD)
+        return pl.ds(h * HEAD if isinstance(h, int) else pl.multiple_of(h * HEAD, HEAD), HEAD)
 
     def rows_of(b):
         return slice(b * SUB, (b + 1) * SUB)
@@ -274,15 +331,9 @@
     def weigh_queries(h):
         make_down(h)
         for b in range(BLOCKS):
-            weighted[rows_of(b), lanes(h)] = (
-                q[rows_of(b), lanes(h)].astype(F32) * down(h, b)
-            ).astype(BF16)
+            weighted_q = q[rows_of(b), lanes(h)].astype(F32) * down(h, b)
+            weighted[h, :, rows_of(b)] = weighted_q.T.astype(BF16)
             rest_weight[h, rows_of(b)] = up(h, b, 1)
-
-    def add_remote(h):
-        remote = dot(q[:, lanes(h)], incoming[pl.ds(h * HEAD, HEAD)], 1, 0)
-        for b in range(BLOCKS):
-            attn[rows_of(b), lanes(h)] += down(h, b, 1) * remote[rows_of(b)]
 
     def send_row(source, target, kind, peer_ctx):
         pltpu.make_async_remote_copy(
@@ -296,23 +347,39 @@
 
     lane = lax.broadcasted_iota(jnp.int32, (1, HEAD), 1)
 
-    def gather_gain():
+    def sum_of(ref):
+        total = ref[0]
+        for n in range(1, ref.shape[0]):
+            total = total + ref[n]
+        return total
+
+    def sum_near(ref, kind):
+        for n in range(1, WINDOW):
+            send_row(ref.at[0], ref.at[n], kind, x * Z + ring(NEAR[n]))
+
+    def sum_far(ref, kind):
+        for n, b in enumerate(far_steps):
+            send_row(ref.at[0], ref.at[n + 1], kind, x * Z + ring(b))
+
+    def rows_arrived(ref, sem):
+        wait_for(ref.at[pl.ds(0, ref.shape[0] - 1)], small_sems.at[sem])
+
+    def gain_first():
         own = jnp.zeros((1, HEAD), F32)
         for n in range(share):
             own = jnp.where(lane == z * share + n, gain_ref[n], own)
-        gain_z[z] = own
-        each_peer(Z, z, lambda peer: send_row(gain_z.at[z], gain_z.at[z], 0, x * Z + peer))
-
-    def spread_gain():
-        wait_for(gain_z.at[pl.ds(0, Z - 1)], small_sems.at[1])
-        whole = gain_z[0]
-        for n in range(1, Z):
-            whole = whole + gain_z[n]
-        gain_x[x] = whole
-        each_peer(X, x, lambda peer: send_row(gain_x.at[x], gain_x.at[x], 2, peer * Z + z))
-
-    def gain_arrived():
-        wait_for(gain_x.at[pl.ds(0, X - 1)], small_sems.at[3])
+        gain_near[0] = own
+        sum_near(gain_near, 0)
+
+    def gain_second():
+        rows_arrived(gain_near, 1)
+        gain_far[0] = sum_of(gain_near)
+        sum_far(gain_far, 2)
+
+    def gain_third():
+        rows_arrived(gain_far, 3)
+        gain_x[x] = sum_of(gain_far)
+        each_peer(X, x, lambda peer: send_row(gain_x.at[x], gain_x.at[x], 4, peer * Z + z))
 
     small_loads[0].wait()
     for h in range(LOCAL):
@@ -322,49 +389,63 @@
     for h in range(LOCAL):
         block_state(h)
     small_loads[1].wait()
-    pl.semaphore_wait(barrier, (Z - 1) + (X - 1) + (DP - 1))
+    pl.semaphore_wait(barrier, len(near) + DP - 1)
+    tell(0, 2)
+    gain_first()
     ahead.exchange()
-    gather_gain()
     loaded(2)
-    for h in range(LOCAL):
-        local_part(h)
+    local_part(0)
+    told(0)
+    tell(1, 4)
+    local_part(1)
+    told(1)
+    gain_second()
+    ahead.total()
+    local_part(2)
+    local_part(3)
     for h in range(LOCAL):
         weigh_queries(h)
     loaded(3)
-    ahead.total()
-    spread_gain()
     ahead.finish()
-    gain_arrived()
+    gain_third()
+    rows_arrived(gain_x, 5)
+    for h in range(LOCAL):
+        for b in range(BLOCKS):
+            at = (rows_of(b), lanes(h))
+            cot_gain[at] = cot[at].astype(F32) * gain_x[h]
+    factors = [[scaled(h, SUB * b + 1) for b in range(BLOCKS)] for h in range(LOCAL)]
     ahead.arrived()
-    for h in range(LOCAL):
-        add_remote(h)
-
-    ones = jnp.ones((8, HEAD), F32)
+
+    remote = [
+        dot(q[:, lanes(h)], incoming[pl.ds(h * HEAD, HEAD)], 1, 0) for h in range(LOCAL)
+    ]
     row8 = lax.broadcasted_iota(jnp.int32, (8, HEAD), 0)
     sums = jnp.zeros((8, HEAD), F32)
     for b in range(BLOCKS):
         square = jnp.zeros((SUB, HEAD), F32)
         cross = jnp.zeros((SUB, HEAD), F32)
         for h in range(LOCAL):
-            a = attn[rows_of(b), lanes(h)]
+            at = (rows_of(b), lanes(h))
+            a = attn[at] + down_base[h] * factors[h][b] * remote[h][rows_of(b)]
+            attn[at] = a
             square = square + a * a
-            cross = cross + cot[rows_of(b), lanes(h)].astype(F32) * gain_x[h] * a
-        sums = jnp.where(row8 == b, dot(ones, square, 1, 1, HIGH), sums)
-        sums = jnp.where(row8 == b + BLOCKS, dot(ones, cross, 1, 1, HIGH), sums)
+            cross = cross + cot_gain[at] * a
+        sums = jnp.where(row8 == b, jnp.sum(square.T, axis=0, keepdims=True), sums)
+        sums = jnp.where(row8 == b + BLOCKS, jnp.sum(cross.T, axis=0, keepdims=True), sums)
     norm_parts[d] = sums
 
     def send_norm(peer):
         pltpu.make_async_remote_copy(
             src_ref=norm_parts.at[d],
             dst_ref=norm_parts.at[d],
-            send_sem=small_sems.at[4],
-            recv_sem=small_sems.at[5],
+            send_sem=small_sems.at[12],
+            recv_sem=small_sems.at[13],
             device_id={"dp": peer},
             device_id_type=MESH,
         ).start()
 
     each_peer(DP, d, send_norm)
-    wait_for(norm_parts.at[pl.ds(0, DP - 1)], small_sems.at[5])
+    rows_arrived(norm_parts, 13)
     whole = norm_parts[0]
     for n in range(1, DP):
         whole = whole + norm_parts[n]
@@ -381,10 +462,10 @@
         for b in range(BLOCKS):
             at = (rows_of(b), lanes(h))
             grad[at] = (
-                cot[at].astype(F32) * gain_x[h] * inverse[b] - attn[at] * cross_part[b]
+                cot_gain[at] * inverse[b] - attn[at] * cross_part[b]
             ).astype(BF16)
-        state = dot(weighted[:, lanes(h)], grad[:, lanes(h)], 0, 0)
-        behind.send[pl.ds(h * HEAD, HEAD)] = state.astype(BF16)
+        state = dot(weighted[h], grad[:, lanes(h)], 1, 0)
+        behind.send[pl.ds(pl.multiple_of(h * HEAD, HEAD), HEAD)] = state.astype(BF16)
 
     def norm_out(h):
         total = jnp.zeros((1, HEAD), F32)
@@ -399,19 +480,19 @@
         each_peer(X, x, lambda peer: send_row(term.at[peer], term_x.at[x], 6, peer * Z + z))
         term_x[x] = term[x]
 
-    def gather_term():
-        wait_for(term_x.at[pl.ds(0, X - 1)], small_sems.at[7])
-        whole = term_x[0]
-        for n in range(1, X):
-            whole = whole + term_x[n]
-        term_z[z] = whole
-        each_peer(Z, z, lambda peer: send_row(term_z.at[z], term_z.at[z], 8, x * Z + peer))
+    def term_second():
+        rows_arrived(term_x, 7)
+        term_near[0] = sum_of(term_x)
+        sum_near(term_near, 8)
+
+    def term_third():
+        rows_arrived(term_near, 9)
+        term_far[0] = sum_of(term_near)
+        sum_far(term_far, 10)
 
     def finish_term():
-        wait_for(term_z.at[pl.ds(0, Z - 1)], small_sems.at[9])
-        whole = term_z[0]
-        for n in range(1, Z):
-            whole = whole + term_z[n]
+        rows_arrived(term_far, 11)
+        whole = sum_of(term_far)
         source = lax.broadcasted_iota(jnp.int32, (HEAD, HEAD), 0)
         target = lax.broadcasted_iota(jnp.int32, (HEAD, HEAD), 1)
         pick = (source == target + z * share).astype(F32)
@@ -434,18 +515,21 @@
         gv_part[0:HALF, lanes(h)] = first
         gv_part[HALF:TOK, lanes(h)] = second
 
-    for h in range(LOCAL):
+    for a in (2, 1, 3, 0):
+        h = lax.rem(x + a, LOCAL)
         back_state(h)
-    behind.exchange()
+        behind.exchange_with(a)
+    behind.keep()
     for h in range(LOCAL):
         norm_out(h)
     spread_term()
     gradient_part(0)
     gradient_part(1)
-    gather_term()
+    behind.total()
+    term_second()
     gradient_part(2)
     gradient_part(3)
-    behind.total()
+    term_third()
     behind.finish()
     finish_term()
     behind.arrived()
@@ -453,11 +537,13 @@
 
     ahead.close()
     behind.close()
-    wait_for(gain_z.at[pl.ds(0, Z - 1)], small_sems.at[0])
-    wait_for(gain_x.at[pl.ds(0, X - 1)], small_sems.at[2])
-    wait_for(norm_parts.at[pl.ds(0, DP - 1)], small_sems.at[4])
-    wait_for(term_x.at[pl.ds(0, X - 1)], small_sems.at[6])
-    wait_for(term_z.at[pl.ds(0, Z - 1)], small_sems.at[8])
+    rows_arrived(gain_near, 0)
+    rows_arrived(gain_far, 2)
+    rows_arrived(gain_x, 4)
+    rows_arrived(term_x, 6)
+    rows_arrived(term_near, 8)
+    rows_arrived(term_far, 10)
+    rows_arrived(norm_parts, 12)
 
 
 def writer(
@@ -503,16 +589,19 @@
 
 
 def per_device(Z, DP, queries, keys, values, cotangent, log_decay, gain):
-    rows = WIDE // Z
+    owners = Z // WINDOW
     share = gain.shape[0]
     tokens = pltpu.VMEM((TOK, WIDE), BF16)
     square = pltpu.VMEM((LOCAL, TOK, TOK), BF16)
     scan = [
         pltpu.VMEM((WIDE, HEAD), BF16),
-        pltpu.VMEM((Z, rows, HEAD), BF16),
-        pltpu.VMEM((Z, rows, HEAD), F32),
-        pltpu.VMEM((X, rows, HEAD), F32),
-        pltpu.VMEM((Z, rows, HEAD), BF16),
+        pltpu.VMEM((WINDOW, X + 2, PIECE, HEAD), BF16),
+        pltpu.VMEM((X + 1, WINDOW, PIECE, HEAD), F32),
+        pltpu.VMEM((X + 3, PIECE, HEAD), F32),
+        pltpu.VMEM((X + 1, PIECE, HEAD), BF16),
+        pltpu.VMEM((owners - 1, X + 3, PIECE, HEAD), BF16),
+        pltpu.VMEM((X + 1, PIECE, HEAD), F32),
+        pltpu.VMEM((X, WINDOW, PIECE, HEAD), BF16),
         pltpu.VMEM((WIDE, HEAD), BF16),
         pltpu.SemaphoreType.DMA((6,)),
     ]
@@ -544,23 +633,26 @@
             tokens,
             tokens,
             tokens,
-            tokens,
+            pltpu.VMEM((LOCAL, HEAD, TOK), BF16),
             square,
             square,
             pltpu.VMEM((LOCAL, 2, HALF, HALF), F32),
             pltpu.VMEM((LOCAL, SUB, HEAD), F32),
             pltpu.VMEM((LOCAL, SUB, HEAD), F32),
             pltpu.VMEM((TOK, WIDE), F32),
+            pltpu.VMEM((TOK, WIDE), F32),
             pltpu.VMEM((DP, 8, HEAD), F32),
-            pltpu.VMEM((Z, 1, HEAD), F32),
+            pltpu.VMEM((WINDOW, 1, HEAD), F32),
+            pltpu.VMEM((owners, 1, HEAD), F32),
             pltpu.VMEM((X, 1, HEAD), F32),
             pltpu.VMEM((LOCAL, 1, HEAD), F32),
             pltpu.VMEM((X, 1, HEAD), F32),
-            pltpu.VMEM((Z, 1, HEAD), F32),
+            pltpu.VMEM((WINDOW, 1, HEAD), F32),
+            pltpu.VMEM((owners, 1, HEAD), F32),
         ]
         + scan
         + scan
-        + [pltpu.SemaphoreType.DMA((6,)), pltpu.SemaphoreType.DMA((10,))],
+        + [pltpu.SemaphoreType.DMA((6,)), pltpu.SemaphoreType.DMA((14,)), pltpu.SemaphoreType.REGULAR((2,))],
         compiler_params=pltpu.CompilerParams(
             collective_id=0, has_side_effects=True, vmem_limit_bytes=40 * 1024 * 1024
         ),

time: 63.9 us -> 61 us (0.955)
  the two profiles are of different devices: /device:TPU:2 before, /device:TPU:64 now
where the time goes in v3:
time: 61 us; the launch traced here: 60.9 us
  Pallas kernels  60.2 us (99%)
  between operations  0.64 us (1%)
    pallas_call x1, Pallas kernels, per_device(): pl.pallas_call(functools.partial(kernel, Z, DP), out_shape=[half, half, h...  58.9 us
    pallas_call x1, Pallas kernels, per_device(): pl.pallas_call(writer, out_shape=[half, half, half, half, jax.ShapeDtypeS...  1.35 us

profile of v3, /device:TPU:64, one launch (start us, length us, event | category | flops | bytes accessed | tf_op | source)
XLA Modules:
  0.0 60.9 jit_solution(8088831343262319641)
XLA Ops:
  0.6 58.9 %shard_map.101 = (bf16[512,512]{1,0:T(8,128)(2,1)S(1)}, bf16[512,512]{1,0:T(8,128)(2,1)S(1)}, bf16[512,512]{1,0:T(8,128)(2,1)S(1)}, bf16[512,512]{1,0:T(8,128)(2...) custom-call(f32[4]{0:T(128)} %rate_hbm.1, ...), custom_call_target="tpu_custom_call" | custom-call | flops 2000000000 | bytes 4200000 | tf_op jit(solution)/shard_map/pallas_call | solution.py:615
  59.5 1.3 %shard_map.102 = (bf16[512,512]{1,0:T(8,128)(2,1)}, bf16[512,512]{1,0:T(8,128)(2,1)}, bf16[512,512]{1,0:T(8,128)(2,1)}, bf16[512,512]{1,0:T(8,128)(2,1)}, f32[1,8]{1,0:T(1,128)}) custom-call(bf16[512,512]{1,0:T(8,128)(2,1)S(1)} %get-tuple-element.19.k, bf16[512,512]{1,0:T(8,128)(2,1)S(1)} %get-tuple-element.20.v, ...), custom_call_target="tpu_custom_call" | custom-call | flops 300000000 | bytes 2200000 | tf_op jit(solution)/shard_map/pallas_call | solution.py:663

commit v4 on v3

--- a/solution.py
+++ b/solution.py
@@ -391,16 +391,16 @@
     small_loads[1].wait()
     pl.semaphore_wait(barrier, len(near) + DP - 1)
     tell(0, 2)
+    ahead.exchange()
     gain_first()
-    ahead.exchange()
     loaded(2)
     local_part(0)
     told(0)
     tell(1, 4)
     local_part(1)
     told(1)
+    ahead.total()
     gain_second()
-    ahead.total()
     local_part(2)
     local_part(3)
     for h in range(LOCAL):

time: 61 us -> 61.2 us (level)
  no operation moved by 1% of the time
where the time goes in v4:
time: 61.2 us; the launch traced here: 61.1 us
  Pallas kernels  60.4 us (99%)
  between operations  0.64 us (1%)
    pallas_call x1, Pallas kernels, per_device(): pl.pallas_call(functools.partial(kernel, Z, DP), out_shape=[half, half, h...  59.1 us
    pallas_call x1, Pallas kernels, per_device(): pl.pallas_call(writer, out_shape=[half, half, half, half, jax.ShapeDtypeS...  1.35 us

profile of v4, /device:TPU:64, one launch (start us, length us, event | category | flops | bytes accessed | tf_op | source)
XLA Modules:
  0.0 61.1 jit_solution(9444466816189680611)
XLA Ops:
  0.6 59.1 %shard_map.101 = (bf16[512,512]{1,0:T(8,128)(2,1)S(1)}, bf16[512,512]{1,0:T(8,128)(2,1)S(1)}, bf16[512,512]{1,0:T(8,128)(2,1)S(1)}, bf16[512,512]{1,0:T(8,128)(2...) custom-call(f32[4]{0:T(128)} %rate_hbm.1, ...), custom_call_target="tpu_custom_call" | custom-call | flops 2000000000 | bytes 4200000 | tf_op jit(solution)/shard_map/pallas_call | solution.py:615
  59.7 1.3 %shard_map.102 = (bf16[512,512]{1,0:T(8,128)(2,1)}, bf16[512,512]{1,0:T(8,128)(2,1)}, bf16[512,512]{1,0:T(8,128)(2,1)}, bf16[512,512]{1,0:T(8,128)(2,1)}, f32[1,8]{1,0:T(1,128)}) custom-call(bf16[512,512]{1,0:T(8,128)(2,1)S(1)} %get-tuple-element.19.k, bf16[512,512]{1,0:T(8,128)(2,1)S(1)} %get-tuple-element.20.v, ...), custom_call_target="tpu_custom_call" | custom-call | flops 300000000 | bytes 2200000 | tf_op jit(solution)/shard_map/pallas_call | solution.py:663
